TPU v7x, 32 devices: a whole 2x2x4 slice. The times are simulated.
32 devices in a mesh: dp: 16 (over z, y, core), mp: 2 (over x).
Axes of the slice: x: 2, y: 2, z: 4, core: 2. Of those that a mesh axis runs over, the one named last changes fastest.
Arguments:
- frames: bfloat16 [32, 320, 768], P('dp', None, 'mp'), may hold values from -16 to 16
- segment_ids: int32 [32, 320], P('dp'), may hold values from 0 to 4, as said below
- live: int32 [32, 320], P('dp'), may hold values from 0 to 1, as said below
- conv_weight: bfloat16 [6144, 768], P('dp', 'mp'), may hold values from -0.078125 to 0.078125
- qkv_weight: bfloat16 [768, 3, 768], P('dp', None, 'mp'), may hold values from -0.3125 to 0.3125
- out_weight: bfloat16 [768, 768], P('mp', 'dp'), may hold values from -0.875 to 0.875
- up_weight: bfloat16 [768, 3072], P('dp', 'mp'), may hold values from -0.21875 to 0.21875
- down_weight: bfloat16 [3072, 768], P('mp', 'dp'), may hold values from -0.109375 to 0.109375
- up_bias: float32 [3072], P('mp'), may hold values from -3 to 3
- gains: float32 [3, 768], P(None, 'mp'), may hold values from 0.1 to 1.9
- biases: float32 [8, 768], P(None, 'mp'), may hold values from -3 to 3
- out_grad: bfloat16 [32, 320, 768], P('dp', None, 'mp'), may hold values from -6 to 6
Outputs:
- mixed: bfloat16 [32, 320, 768], P('dp', None, 'mp')
- grad_frames: float32 [32, 320, 768], P('dp', None, 'mp')
- grad_conv: float32 [6144, 768], P('dp', 'mp')
- grad_qkv: float32 [768, 3, 768], P('dp', None, 'mp')
- grad_out: float32 [768, 768], P('mp', 'dp')
- grad_up: float32 [768, 3072], P('dp', 'mp')
- grad_down: float32 [3072, 768], P('mp', 'dp')
- grad_up_bias: float32 [3072], P('mp')
- grad_gains: float32 [3, 768], P(None, 'mp')
- grad_biases: float32 [8, 768], P(None, 'mp')
Inputs may be any that keep to these rules, and one draw needn't show every extreme that they name: `segment_ids`: along each row the ids start at 0 and never fall; a row holds 2 to 4 clips, each with its own id; padding frames, at the row's end, take the id after the last clip's. `live`: 1 exactly on the frames of clips, 0 on the padding at a row's end.
All inputs are finite; a program needn't handle non-finite values.
Results may differ from a plain program's by a relative error of at most 0.02.
Values may be sent and summed in bfloat16 or wider, within the bound.
A program may use at most 192 MiB of HBM per device.

v0:
```python
from functools import partial

import jax
import jax.numpy as jnp
from jax import lax
from jax.sharding import PartitionSpec as P

D = 768
HEAD_DIM = 64
KERNEL = 128
GROUPS = 16
ROWS_MB = 1
MICRO = 2


EPSILON = 1e-05
MASKED = -1e30


def fetch(conv_weight, qkv_weight, up_weight, out_weight, down_weight):
    return (
        lax.all_gather(conv_weight, "dp", axis=0, tiled=True),
        lax.all_gather(qkv_weight, "dp", axis=0, tiled=True),
        lax.all_gather(up_weight, "dp", axis=0, tiled=True),
        lax.all_gather(out_weight, "dp", axis=1, tiled=True),
        lax.all_gather(down_weight, "dp", axis=1, tiled=True),
    )


def spread_features(features):
    return lax.all_gather(features.astype(jnp.bfloat16), "mp", axis=2, tiled=True)


def spread_grads(features):
    return lax.all_gather(features.astype(jnp.bfloat16), "mp", axis=2, tiled=True)


def fold_partials(features):
    return lax.psum_scatter(
        features.astype(jnp.bfloat16), "mp", scatter_dimension=2, tiled=True
    ).astype(jnp.float32)


def fold_grads(features):
    return lax.psum_scatter(
        features.astype(jnp.bfloat16), "mp", scatter_dimension=2, tiled=True
    ).astype(jnp.float32)


def norm_forward(features, gain_vec, shift_vec):
    row_total = lax.psum(jnp.sum(features, axis=-1), "mp")
    center = features - (row_total / D)[..., None]
    spread = lax.psum(jnp.sum(center * center, axis=-1), "mp")
    variance = spread / D
    inv_scale = lax.rsqrt(variance + EPSILON)[..., None]
    normed = center * inv_scale
    return (normed * gain_vec + shift_vec, normed, inv_scale)


def norm_backward(incoming, normed, inv_scale, gain_vec):
    scaled = incoming * gain_vec
    first_sum, second_sum = lax.psum(
        (jnp.sum(scaled, axis=-1), jnp.sum(scaled * normed, axis=-1)), "mp"
    )
    result = inv_scale * (
        scaled - (first_sum / D)[..., None] - normed * (second_sum / D)[..., None]
    )
    return (result, jnp.sum(incoming * normed, axis=(0, 1)), jnp.sum(incoming, axis=(0, 1)))


def conv_forward(inputs, kernel, group_count):
    tap_count = kernel.shape[0]
    return lax.conv_general_dilated(
        inputs,
        kernel,
        (1,),
        [(tap_count // 2, tap_count // 2 - 1)],
        dimension_numbers=("NWC", "WIO", "NWC"),
        feature_group_count=group_count,
        preferred_element_type=jnp.float32,
    )


def conv_input_grad(grad_low, kernel, group_count):
    tap_count, group_width, channels = kernel.shape
    turned = (
        kernel.reshape(tap_count, group_width, group_count, group_width)
        .transpose(0, 3, 2, 1)
        .reshape(tap_count, group_width, channels)[::-1]
    )
    return lax.conv_general_dilated(
        grad_low,
        turned,
        (1,),
        [(tap_count // 2 - 1, tap_count // 2)],
        dimension_numbers=("NWC", "WIO", "NWC"),
        feature_group_count=group_count,
        preferred_element_type=jnp.float32,
    )


def conv_weight_grad(inputs, grad_low, tap_count, group_count):
    padded = jnp.pad(inputs, ((0, 0), (tap_count // 2, tap_count // 2 - 1), (0, 0)))
    left_side = padded.transpose(2, 1, 0)
    right_side = grad_low.transpose(1, 0, 2)
    weight_grad = lax.conv_general_dilated(
        left_side,
        right_side,
        (1,),
        [(0, 0)],
        dimension_numbers=("NWC", "WIO", "NWC"),
        batch_group_count=group_count,
        preferred_element_type=jnp.float32,
    )
    return weight_grad.transpose(1, 0, 2).reshape(-1, weight_grad.shape[2])


def heads_first(features):
    row_count, frame_count, width = features.shape
    return (
        features.reshape(row_count, frame_count, width // HEAD_DIM, HEAD_DIM)
        .transpose(0, 2, 1, 3)
        .reshape(-1, frame_count, HEAD_DIM)
    )


def heads_last(items, row_count):
    item_count, frame_count, head_width = items.shape
    return (
        items.reshape(row_count, item_count // row_count, frame_count, head_width)
        .transpose(0, 2, 1, 3)
        .reshape(row_count, frame_count, -1)
    )


def masked_scores(queries, keys_low, clip_ids):
    scale_factor = queries.shape[-1] ** (-0.5)
    scores = (
        jnp.einsum("qe,ke->qk", queries, keys_low, preferred_element_type=jnp.float32)
        * scale_factor
    )
    same_clip = clip_ids[:, None] == clip_ids[None, :]
    return jnp.where(same_clip, scores, MASKED)


def attend_one(item_pack):
    queries, keys_low, values, clip_ids = item_pack
    scores = masked_scores(queries, keys_low, clip_ids)
    row_max = jnp.max(scores, axis=-1, keepdims=True)
    weights = jnp.exp(scores - row_max)
    row_total = jnp.sum(weights, axis=-1, keepdims=True)
    probabilities = (weights / row_total).astype(jnp.bfloat16)
    context = jnp.dot(probabilities, values, preferred_element_type=jnp.float32).astype(
        jnp.bfloat16
    )
    return (context, (row_max + jnp.log(row_total))[:, 0])


def attend_back(item_pack):
    queries, keys_low, values, clip_ids, log_total, grad_context = item_pack
    scale_factor = queries.shape[-1] ** (-0.5)
    scores = masked_scores(queries, keys_low, clip_ids)
    probabilities = jnp.exp(scores - log_total[:, None])
    grad_probs = jnp.einsum("qe,ke->qk", grad_context, values, preferred_element_type=jnp.float32)
    row_dot = jnp.sum(grad_probs * probabilities, axis=-1, keepdims=True)
    grad_scores = (probabilities * (grad_probs - row_dot)).astype(jnp.bfloat16)
    grad_queries = (
        jnp.dot(grad_scores, keys_low, preferred_element_type=jnp.float32) * scale_factor
    ).astype(jnp.bfloat16)
    grad_keys = (
        jnp.einsum("qk,qe->ke", grad_scores, queries, preferred_element_type=jnp.float32)
        * scale_factor
    ).astype(jnp.bfloat16)
    grad_values = jnp.einsum(
        "qk,qe->ke",
        probabilities.astype(jnp.bfloat16),
        grad_context,
        preferred_element_type=jnp.float32,
    ).astype(jnp.bfloat16)
    return (grad_queries, grad_keys, grad_values)


def body(
    frames,
    segment_ids,
    live,
    conv_weight,
    qkv_weight,
    out_weight,
    up_weight,
    down_weight,
    up_bias,
    gains,
    biases,
    out_grad,
):
    row_count = ROWS_MB
    local_width = frames.shape[2]
    head_count = local_width // HEAD_DIM
    group_count = local_width // (D // GROUPS)
    gelu_exact = partial(jax.nn.gelu, approximate=False)
    shard_list = (conv_weight, qkv_weight, up_weight, out_weight, down_weight)
    gathered = None
    mixed_parts = []
    input_grads = []
    weight_sums = None
    gain_sums = None
    bias_sums = None
    up_bias_sum = None
    for micro_index in range(MICRO):
        gathered = fetch(*shard_list)
        conv_full, qkv_full, up_full, out_full, down_full = gathered
        kernel = conv_full.reshape(KERNEL, D // GROUPS, local_width)
        row_start = micro_index * row_count
        row_frames = frames[row_start : row_start + row_count]
        clip_ids = segment_ids[row_start : row_start + row_count]
        alive_mask = live[row_start : row_start + row_count]
        masked_input = row_frames * alive_mask.astype(jnp.bfloat16)[..., None]
        conv_out = conv_forward(masked_input, kernel, group_count) + biases[0]
        positioned = row_frames.astype(jnp.float32) + gelu_exact(conv_out)
        first_norm, normed_zero, scale_zero = norm_forward(positioned, gains[0], biases[1])
        first_full = spread_features(first_norm)
        projected = jnp.einsum(
            "rsd,dcn->rscn", first_full, qkv_full, preferred_element_type=jnp.float32
        )
        query_items = heads_first((projected[:, :, 0] + biases[2]).astype(jnp.bfloat16))
        key_items = heads_first(projected[:, :, 1].astype(jnp.bfloat16))
        value_items = heads_first((projected[:, :, 2] + biases[3]).astype(jnp.bfloat16))
        item_ids = jnp.repeat(clip_ids, head_count, axis=0)
        context_items, log_total = lax.map(
            attend_one, (query_items, key_items, value_items, item_ids)
        )
        context = heads_last(context_items, row_count)
        attended = fold_partials(
            jnp.einsum("rsh,hd->rsd", context, out_full, preferred_element_type=jnp.float32)
        )
        second_norm, normed_one, scale_one = norm_forward(
            first_norm + attended + biases[4], gains[1], biases[5]
        )
        second_full = spread_features(second_norm)
        up_proj = (
            jnp.einsum("rsd,df->rsf", second_full, up_full, preferred_element_type=jnp.float32)
            + up_bias
        )
        hidden = gelu_exact(up_proj).astype(jnp.bfloat16)
        down_proj = fold_partials(
            jnp.einsum("rsf,fd->rsd", hidden, down_full, preferred_element_type=jnp.float32)
        )
        mixed_out, normed_two, scale_two = norm_forward(
            second_norm + down_proj + biases[6], gains[2], biases[7]
        )
        mixed_parts.append(mixed_out.astype(jnp.bfloat16))
        incoming = out_grad[row_start : row_start + row_count].astype(jnp.float32)
        grad_second, gain_two, shift_two = norm_backward(incoming, normed_two, scale_two, gains[2])
        grad_down_full = spread_grads(grad_second)
        grad_down = jnp.einsum(
            "rsf,rsd->fd", hidden, grad_down_full, preferred_element_type=jnp.float32
        )
        grad_hidden = jnp.einsum(
            "rsd,fd->rsf", grad_down_full, down_full, preferred_element_type=jnp.float32
        )
        up_pull = jax.vjp(gelu_exact, up_proj)[1]
        grad_up_low = up_pull(grad_hidden)[0].astype(jnp.bfloat16)
        grad_up = jnp.einsum(
            "rsd,rsf->df", second_full, grad_up_low, preferred_element_type=jnp.float32
        )
        grad_up_bias = jnp.sum(grad_up_low, axis=(0, 1), dtype=jnp.float32)
        grad_h_one = grad_second + fold_grads(
            jnp.einsum("rsf,df->rsd", grad_up_low, up_full, preferred_element_type=jnp.float32)
        )
        grad_first, gain_one, shift_one = norm_backward(grad_h_one, normed_one, scale_one, gains[1])
        grad_att_full = spread_grads(grad_first)
        grad_out = jnp.einsum(
            "rsh,rsd->hd", context, grad_att_full, preferred_element_type=jnp.float32
        )
        grad_context = jnp.einsum(
            "rsd,hd->rsh", grad_att_full, out_full, preferred_element_type=jnp.float32
        ).astype(jnp.bfloat16)
        grad_query_items, grad_key_items, grad_value_items = lax.map(
            attend_back,
            (query_items, key_items, value_items, item_ids, log_total, heads_first(grad_context)),
        )
        grad_queries = heads_last(grad_query_items, row_count)
        grad_values = heads_last(grad_value_items, row_count)
        grad_stack = jnp.stack(
            [grad_queries, heads_last(grad_key_items, row_count), grad_values], axis=2
        )
        grad_qkv = jnp.einsum(
            "rsd,rscn->dcn", first_full, grad_stack, preferred_element_type=jnp.float32
        )
        grad_h_zero = grad_first + fold_grads(
            jnp.einsum("rscn,dcn->rsd", grad_stack, qkv_full, preferred_element_type=jnp.float32)
        )
        grad_pos, gain_zero, shift_zero = norm_backward(
            grad_h_zero, normed_zero, scale_zero, gains[0]
        )
        conv_pull = jax.vjp(gelu_exact, conv_out)[1]
        grad_conv_low = conv_pull(grad_pos)[0].astype(jnp.bfloat16)
        grad_conv = conv_weight_grad(masked_input, grad_conv_low, KERNEL, group_count)
        input_grads.append(
            grad_pos
            + alive_mask.astype(jnp.float32)[..., None]
            * conv_input_grad(grad_conv_low, kernel, group_count)
        )
        weight_terms = (grad_conv, grad_qkv, grad_up, grad_out, grad_down)
        gain_terms = jnp.stack([gain_zero, gain_one, gain_two])
        bias_terms = jnp.stack(
            [
                jnp.sum(grad_conv_low, axis=(0, 1), dtype=jnp.float32),
                shift_zero,
                jnp.sum(grad_queries, axis=(0, 1), dtype=jnp.float32),
                jnp.sum(grad_values, axis=(0, 1), dtype=jnp.float32),
                jnp.sum(grad_first, axis=(0, 1)),
                shift_one,
                jnp.sum(grad_second, axis=(0, 1)),
                shift_two,
            ]
        )
        if weight_sums is None:
            weight_sums, gain_sums, bias_sums, up_bias_sum = (
                weight_terms,
                gain_terms,
                bias_terms,
                grad_up_bias,
            )
        else:
            weight_sums = tuple(
                (running + addend for running, addend in zip(weight_sums, weight_terms))
            )
            gain_sums = gain_sums + gain_terms
            bias_sums = bias_sums + bias_terms
            up_bias_sum = up_bias_sum + grad_up_bias
    conv_part, qkv_part, up_part, out_part, down_part = (
        lax.psum_scatter(weight_sums[0], "dp", scatter_dimension=0, tiled=True),
        lax.psum_scatter(weight_sums[1], "dp", scatter_dimension=0, tiled=True),
        lax.psum_scatter(weight_sums[2], "dp", scatter_dimension=0, tiled=True),
        lax.psum_scatter(weight_sums[3], "dp", scatter_dimension=1, tiled=True),
        lax.psum_scatter(weight_sums[4], "dp", scatter_dimension=1, tiled=True),
    )
    gain_total, bias_total, up_bias_total = lax.psum((gain_sums, bias_sums, up_bias_sum), "dp")
    mixed_all = jnp.concatenate(mixed_parts, axis=0)
    grad_all = jnp.concatenate(input_grads, axis=0)
    return (
        mixed_all,
        grad_all,
        conv_part,
        qkv_part,
        out_part,
        up_part,
        down_part,
        up_bias_total,
        gain_total,
        bias_total,
    )


def solution(mesh):
    placed = (
        P("dp", None, "mp"),
        P("dp", None),
        P("dp", None),
        P("dp", "mp"),
        P("dp", None, "mp"),
        P("mp", "dp"),
        P("dp", "mp"),
        P("mp", "dp"),
        P("mp"),
        P(None, "mp"),
        P(None, "mp"),
        P("dp", None, "mp"),
    )
    return jax.shard_map(
        body,
        mesh=mesh,
        in_specs=placed,
        out_specs=(
            P("dp", None, "mp"),
            P("dp", None, "mp"),
            P("dp", "mp"),
            P("dp", None, "mp"),
            P("mp", "dp"),
            P("dp", "mp"),
            P("mp", "dp"),
            P("mp"),
            P(None, "mp"),
            P(None, "mp"),
        ),
        check_vma=False,
    )
```

profile of v0, /device:TPU:0, one launch (start us, length us, event | category | flops | bytes accessed | tf_op | source)
XLA Modules:
  0.0 1756.0 jit_solution(9363647060426025641)
XLA Ops:
  16.9 27.0 %all_gather.47 = bf16[384,768]{0,1:T(8,128)(2,1)} all-gather(bf16[384,48]{0,1:T(8,128)(2,1)S(1)} %copy-done.93), channel_id=1, replica_groups=mesh['dp'=16,'mp'=2] {'dp'}, dimensions={1}, use_global_device_ids=true | all-gather | bytes 626688 | tf_op jit(solution)/shard_map/all_gather | solution.py:25
  47.4 20.6 %all-gather.5.cloned.1.call-done = bf16[6144,384]{1,0:T(8,128)(2,1)} async-done(((bf16[384,384]{1,0:T(8,128)(2,1)}), bf16[6144,384]{1,0:T(8,128)(2,1)}) %all-gather.5.cloned.1.call-update) | async-done | bytes 4718608 | tf_op jit(solution)/shard_map/all_gather | solution.py:22
  68.0 17.3 reshape.1579
  85.3 82.6 %fusion.92 = f32[1,320,8,48]{3,0,2,1:T(1,128)} fusion(bf16[1,320,8,48]{3,0,2,1:T(2,128)(2,1)S(1)} %copy.172, bf16[128,48,8,48]{3,2,1,0:T(8,128)(2,1)} %reshape.1579), kind=kOutput, calls=%fused_computation.120 | convolution fusion | flops 1358954496 | bytes 5455872 | tf_op jit(solution)/shard_map/conv_general_dilated | solution.py:73
  167.9 83.4 %fusion.94 = f32[1,320,8,48]{3,0,2,1:T(1,128)} fusion(bf16[1,320,8,48]{3,0,2,1:T(2,128)(2,1)} %copy.161, bf16[128,48,8,48]{3,2,1,0:T(8,128)(2,1)} %reshape.1579), kind=kOutput, calls=%fused_computation.122 | convolution fusion | flops 1358954496 | bytes 5455872 | tf_op jit(solution)/shard_map/conv_general_dilated | solution.py:73
  258.7 4.9 all-reduce.11
  264.0 4.9 all-reduce.10
  269.3 6.9 all_gather.51
  279.6 6.9 all_gather.45
  300.8 15.1 while.52
  322.3 15.1 while.53
  346.5 10.4 reduce-scatter.44.cloned.1.call-done
  359.3 4.9 all-reduce.9
  364.8 4.9 all-reduce.8
  370.1 7.1 all_gather.48
  377.2 7.0 all_gather.52
  384.2 17.1 all-gather.9.cloned.1.call-done
  401.3 7.6 multiply_convert_fusion.2
  409.0 35.5 %all-gather.11.cloned.1.call-done = bf16[1536,768]{0,1:T(8,128)(2,1)} async-done(((bf16[1536,48]{0,1:T(8,128)(2,1)}), bf16[1536,768]{0,1:T(8,128)(2,1)}) %all-gather.11.cloned.1.call-update) | async-done | bytes 2359312 | tf_op jit(solution)/shard_map/all_gather | solution.py:26
  447.9 4.6 copy.225
  454.8 8.0 multiply_convert_fusion.3
  472.6 14.5 reduce-scatter.42.cloned.1.call-done
  492.7 5.6 all-reduce.7
  501.4 5.6 all-reduce.6
  512.9 5.9 all-reduce.5
  524.4 6.9 all_gather.55
  531.2 4.4 convert_reduce_fusion
  542.7 6.9 all_gather.53
  549.5 5.1 convert_reduce_fusion.1
  566.5 10.5 reduce-scatter.48.cloned.1.call-done
  584.2 5.0 all-reduce.4
  592.4 7.2 all_gather.54
  601.2 38.2 %while.54 = (s32[]{:T(128)}, bf16[6,320,64]{1,2,0:T(8,128)(2,1)S(1)}, bf16[6,320,64]{1,2,0:T(8,128)(2,1)S(1)}, bf16[6,320,64]{1,2,0:T(8,128)(2,1)S(1)}, s32[6,32...) while((s32[]{:T(128)}, ...), condition=%wide.region_47.48_spmd, body=%wide.region_45.47_spmd.sunk | while | flops 66662080 | bytes 3992189 | solution.py:279
  640.7 6.9 all_gather.56
  657.0 50.4 %while.55 = (s32[]{:T(128)}, bf16[6,320,64]{1,2,0:T(8,128)(2,1)S(1)}, bf16[6,320,64]{1,2,0:T(8,128)(2,1)}, bf16[6,320,64]{1,2,0:T(8,128)(2,1)}, s32[6,320]{1,0:T...) while((s32[]{:T(128)}, ...), condition=%wide.region_64.65_spmd, body=%wide.region_62.64_spmd.sunk | while | flops 66662080 | bytes 3787389 | solution.py:279
  734.9 3.8 copy.211
  738.7 3.9 copy.215
  743.3 21.1 %copy.191 = bf16[128,48,8,48]{0,3,2,1:T(8,128)(2,1)} copy(bf16[128,48,8,48]{1,2,3,0:T(8,128)(2,1)} %bitcast.461) | data formatting | bytes 9437184 | tf_op jit(solution)/shard_map/transpose | solution.py:88
  764.4 70.0 %rev.6 = bf16[128,48,384]{0,2,1:T(8,128)(2,1)} reverse(bf16[128,48,384]{0,2,1:T(8,128)(2,1)} %bitcast.464), dimensions={0} | reverse | bytes 9437184 | tf_op jit(solution)/shard_map/rev | solution.py:87
  834.4 18.0 %copy.193 = bf16[128,48,8,48]{3,1,2,0:T(8,128)(2,1)} copy(bf16[128,48,8,48]{0,3,2,1:T(8,128)(2,1)} %bitcast.465) | data formatting | bytes 9437184 | tf_op jit(solution)/shard_map/rev | solution.py:87
  879.0 5.0 all-reduce.3
  894.1 243.4 %fusion.206 = f32[48,128,8,48]{3,0,2,1:T(8,128)} fusion(bf16[8,48,447,1]{1,3,0,2:T(2,128)(2,1)} %copy.211, bf16[320,1,8,48]{3,1,2,0:T(2,128)(2,1)} %copy.212), kind=kOutput, calls=%fused_computation.417 | convolution fusion | flops 1509949440 | bytes 10026240 | tf_op jit(solution)/shard_map/conv_general_dilated | solution.py:106
  1137.5 252.3 %convolution_add_fusion = f32[48,128,8,48]{3,0,2,1:T(8,128)} fusion(f32[48,128,8,48]{3,0,2,1:T(8,128)} %fusion.206, bf16[8,48,447,1]{1,3,0,2:T(2,128)(2,1)S(1)} %copy-done.55, bf16[320,1,8,48]{3,1,2,0:T(2,128)(2,1)} %copy.216), kind=kOutput, calls=%fused_computation.124 | convolution fusion | flops 1512308736 | bytes 19463424 | tf_op jit(solution)/shard_map/conv_general_dilated | solution.py:106
  1389.8 129.0 %fusion.205 = f32[1,320,8,48]{3,0,2,1:T(1,128)} fusion(bf16[1,320,8,48]{3,0,2,1:T(2,128)(2,1)} %copy.205, bf16[128,48,8,48]{3,1,2,0:T(8,128)(2,1)} %copy.193), kind=kOutput, calls=%fused_computation.416 | convolution fusion | flops 1358954496 | bytes 5455872 | tf_op jit(solution)/shard_map/conv_general_dilated | solution.py:91
  1520.1 20.5 %copy.217 = f32[48,128,8,48]{1,3,2,0:T(8,128)} copy(f32[48,128,8,48]{3,0,2,1:T(8,128)} %convolution_add_fusion) | data formatting | bytes 18874368 | tf_op jit(solution)/shard_map/add | solution.py:328
  1540.5 9.7 copy.218
  1550.3 131.4 %fusion.204 = f32[1,320,8,48]{3,0,2,1:T(1,128)} fusion(bf16[1,320,8,48]{3,0,2,1:T(2,128)(2,1)S(1)} %copy.192, bf16[128,48,8,48]{3,1,2,0:T(8,128)(2,1)} %copy.193), kind=kOutput, calls=%fused_computation.415 | convolution fusion | flops 1358954496 | bytes 5455872 | tf_op jit(solution)/shard_map/conv_general_dilated | solution.py:91
  1688.7 57.7 %all-reduce.2 = (f32[1536]{0:T(1024)}, f32[3,384]{1,0:T(4,128)}, f32[8,384]{1,0:T(8,128)}) all-reduce(f32[1536]{0:T(1024)S(1)} %copy-done.94, f32[3,384]{1,0:T(4,128)S(1)} %maximum_add_fusion, f32[8,384]{1,0:T(8,128)S(1)} %add.496), channel_id=1, replica_groups=mesh['dp'=16,'mp'=2] {'dp'}, use_global_device_ids=true, to_apply=%region_77.78 | all-reduce | flops 5760 | bytes 46080 | tf_op jit(solution)/shard_map/psum | solution.py:340
  (767 shorter events, 326.1 us)
Async XLA Ops:
  7.2 60.8 %all-gather.5.cloned.1.call-start = ((), (), s32[]{:S(2)}) async-start(), calls=%async_computation.13 | async-start | bytes 5013504 | tf_op jit(solution)/shard_map/all_gather | solution.py:22
  7.9 268.3 %all-gather.7.cloned.1.call-start = ((), (), s32[]{:S(2)}) async-start(), calls=%async_computation.14 | async-start | bytes 1880064 | tf_op jit(solution)/shard_map/all_gather | solution.py:23
  8.7 335.9 %reduce-scatter.40.cloned.1.call-start = ((), (), s32[]{:S(2)}) async-start(), calls=%async_computation.22 | async-start | bytes 884736
  167.9 83.4 %copy-start.58 = (f32[1,320,8,48]{3,0,2,1:T(1,128)S(1)}, f32[1,320,8,48]{3,0,2,1:T(1,128)}, u32[]{:S(2)}) copy-start(f32[1,320,8,48]{3,0,2,1:T(1,128)} %fusion.92) | copy-start | bytes 1474564
  258.7 625.5 %copy-start = (f32[1,320,384]{2,1,0:T(8,128)}, f32[1,320,384]{2,1,0:T(8,128)S(1)}, u32[]{:S(2)}) copy-start(f32[1,320,384]{2,1,0:T(8,128)S(1)} %get-tuple-element.479) | copy-start | bytes 1474564
  258.7 625.5 %copy-start.2 = (f32[1,320,384]{2,1,0:T(8,128)}, f32[1,320,384]{2,1,0:T(8,128)S(1)}, u32[]{:S(2)}) copy-start(f32[1,320,384]{2,1,0:T(8,128)S(1)} %get-tuple-element.502) | copy-start | bytes 1474564
  263.7 620.5 %copy-start.74 = (f32[320]{0:T(512)}, f32[320]{0:T(512)S(1)}, u32[]{:S(2)}) copy-start(f32[320]{0:T(512)S(1)} %multiply_reduce_fusion.34) | copy-start | bytes 3844
  263.7 620.5 %copy-start.76 = (f32[320]{0:T(512)}, f32[320]{0:T(512)S(1)}, u32[]{:S(2)}) copy-start(f32[320]{0:T(512)S(1)} %multiply_reduce_fusion.37) | copy-start | bytes 3844
  269.0 615.2 %copy-start.78 = (f32[320]{0:T(512)}, f32[320]{0:T(512)S(1)}, u32[]{:S(2)}) copy-start(f32[320]{0:T(512)S(1)} %rsqrt_reduce_fusion.2) | copy-start | bytes 3844
  269.0 615.2 %copy-start.80 = (f32[320]{0:T(512)}, f32[320]{0:T(512)S(1)}, u32[]{:S(2)}) copy-start(f32[320]{0:T(512)S(1)} %rsqrt_reduce_fusion.5) | copy-start | bytes 3844
  322.2 34.7 %reduce-scatter.44.cloned.1.call-start = ((), (), s32[]{:S(2)}) async-start(), calls=%async_computation.24 | async-start | bytes 884736
  343.0 58.4 %all-gather.9.cloned.1.call-start = ((), (), s32[]{:S(2)}) async-start(), calls=%async_computation.15 | async-start | bytes 2506752 | tf_op jit(solution)/shard_map/all_gather | solution.py:24
  343.6 100.9 %all-gather.11.cloned.1.call-start = ((), (), s32[]{:S(2)}) async-start(), calls=%async_computation.16 | async-start | bytes 2506752 | tf_op jit(solution)/shard_map/all_gather | solution.py:26
  344.1 125.6 %reduce-scatter.46.cloned.1.call-start = ((), (), s32[]{:S(2)}) async-start(), calls=%async_computation.25 | async-start | bytes 884736
  454.7 32.4 %reduce-scatter.42.cloned.1.call-start = ((), (), s32[]{:S(2)}) async-start(), calls=%async_computation.23 | async-start | bytes 884736
  469.7 91.9 %reduce-scatter.52.cloned.1.call-start = ((), (), s32[]{:S(2)}) async-start(), calls=%async_computation.28 | async-start | bytes 884736
  542.6 34.4 %reduce-scatter.48.cloned.1.call-start = ((), (), s32[]{:S(2)}) async-start(), calls=%async_computation.26 | async-start | bytes 884736
  561.5 308.7 %reduce-scatter.50.cloned.1.call-start = ((), (), s32[]{:S(2)}) async-start(), calls=%async_computation.27 | async-start | bytes 884736
  655.2 217.8 %reduce-scatter.54.cloned.1.call-start = ((), (), s32[]{:S(2)}) async-start(), calls=%async_computation.29 | async-start | bytes 884736
  657.0 55.0 %copy-start.6 = (bf16[768,3,384]{2,0,1:T(8,128)(2,1)S(1)}, bf16[768,3,384]{2,0,1:T(8,128)(2,1)}, u32[]{:S(2)}) copy-start(bf16[768,3,384]{2,0,1:T(8,128)(2,1)} %all-gather.7.cloned.1.call-done) | copy-start | bytes 5308420
  719.3 1029.7 %reduce-scatter.34.cloned.1.call-start = ((), (), s32[]{:S(2)}) async-start(), calls=%async_computation.19 | async-start | bytes 1253376 | tf_op jit(solution)/shard_map/reduce_scatter | solution.py:337
  722.7 1026.4 %reduce-scatter.32.cloned.1.call-start = ((), (), s32[]{:S(2)}) async-start(), calls=%async_computation.18 | async-start | bytes 3760128 | tf_op jit(solution)/shard_map/reduce_scatter | solution.py:335
  727.0 1022.0 %reduce-scatter.36.cloned.1.call-start = ((), (), s32[]{:S(2)}) async-start(), calls=%async_computation.20 | async-start | bytes 5013504 | tf_op jit(solution)/shard_map/reduce_scatter | solution.py:336
  733.4 1015.6 %reduce-scatter.38.cloned.1.call-start = ((), (), s32[]{:S(2)}) async-start(), calls=%async_computation.21 | async-start | bytes 5013504 | tf_op jit(solution)/shard_map/reduce_scatter | solution.py:338
  861.5 887.6 %reduce-scatter.30.cloned.1.call-start = ((), (), s32[]{:S(2)}) async-start(), calls=%async_computation.17 | async-start | bytes 10027008 | tf_op jit(solution)/shard_map/reduce_scatter | solution.py:334
  894.1 243.4 %copy-start.55 = (bf16[8,48,447,1]{1,3,0,2:T(2,128)(2,1)S(1)}, bf16[8,48,447,1]{1,3,0,2:T(2,128)(2,1)}, u32[]{:S(2)}) copy-start(bf16[8,48,447,1]{1,3,0,2:T(2,128)(2,1)} %copy.215) | copy-start | bytes 1029892
  1389.8 129.1 %copy-start.40 = (bf16[1,320,384]{1,2,0:T(8,128)(2,1)S(1)}, bf16[1,320,384]{1,2,0:T(8,128)(2,1)}, u32[]{:S(2)}) copy-start(bf16[1,320,384]{1,2,0:T(8,128)(2,1)} %copy-done.39) | copy-start | bytes 737284
  1550.3 131.5 %copy-start.127 = (f32[384]{0:T(512)S(1)}, f32[384]{0:T(512)}, u32[]{:S(2)}) copy-start(f32[384]{0:T(512)} %get-tuple-element.314) | copy-start | bytes 4612
  1550.3 131.5 %copy-start.126 = (f32[384]{0:T(512)S(1)}, f32[384]{0:T(512)}, u32[]{:S(2)}) copy-start(f32[384]{0:T(512)} %get-tuple-element.339) | copy-start | bytes 4612
  1550.3 131.5 %copy-start.125 = (f32[384]{0:T(512)S(1)}, f32[384]{0:T(512)}, u32[]{:S(2)}) copy-start(f32[384]{0:T(512)} %get-tuple-element.522) | copy-start | bytes 4612
  1550.3 131.5 %copy-start.124 = (f32[384]{0:T(512)S(1)}, f32[384]{0:T(512)}, u32[]{:S(2)}) copy-start(f32[384]{0:T(512)} %get-tuple-element.525) | copy-start | bytes 4612
  1550.3 131.5 %copy-start.129 = (f32[384]{0:T(512)S(1)}, f32[384]{0:T(512)}, u32[]{:S(2)}) copy-start(f32[384]{0:T(512)} %get-tuple-element.458) | copy-start | bytes 4612
  1550.3 131.5 %copy-start.128 = (f32[384]{0:T(512)S(1)}, f32[384]{0:T(512)}, u32[]{:S(2)}) copy-start(f32[384]{0:T(512)} %get-tuple-element.510) | copy-start | bytes 4612
  1684.5 61.9 %copy-start.1 = (f32[1,320,384]{2,1,0:T(8,128)S(1)}, f32[1,320,384]{2,1,0:T(8,128)}, u32[]{:S(2)}) copy-start(f32[1,320,384]{2,1,0:T(8,128)} %copy-done) | copy-start | bytes 1474564
  1684.5 61.9 %copy-start.3 = (f32[1,320,384]{2,1,0:T(8,128)S(1)}, f32[1,320,384]{2,1,0:T(8,128)}, u32[]{:S(2)}) copy-start(f32[1,320,384]{2,1,0:T(8,128)} %copy-done.2) | copy-start | bytes 1474564
  1684.5 61.9 %copy-start.20 = (f32[1,320,384]{2,1,0:T(8,128)S(1)}, f32[1,320,384]{2,1,0:T(8,128)}, u32[]{:S(2)}) copy-start(f32[1,320,384]{2,1,0:T(8,128)} %copy-done.19) | copy-start | bytes 1474564
  1684.5 61.9 %copy-start.21 = (f32[1,320,384]{2,1,0:T(8,128)S(1)}, f32[1,320,384]{2,1,0:T(8,128)}, u32[]{:S(2)}) copy-start(f32[1,320,384]{2,1,0:T(8,128)} %get-tuple-element.526) | copy-start | bytes 1474564
  1684.5 61.9 %copy-start.75 = (f32[320]{0:T(512)S(1)}, f32[320]{0:T(512)}, u32[]{:S(2)}) copy-start(f32[320]{0:T(512)} %copy-done.74) | copy-start | bytes 3844
  1684.6 61.9 %copy-start.77 = (f32[320]{0:T(512)S(1)}, f32[320]{0:T(512)}, u32[]{:S(2)}) copy-start(f32[320]{0:T(512)} %copy-done.76) | copy-start | bytes 3844
  1684.6 61.9 %copy-start.79 = (f32[320]{0:T(512)S(1)}, f32[320]{0:T(512)}, u32[]{:S(2)}) copy-start(f32[320]{0:T(512)} %copy-done.78) | copy-start | bytes 3844
  1684.6 61.9 %copy-start.81 = (f32[320]{0:T(512)S(1)}, f32[320]{0:T(512)}, u32[]{:S(2)}) copy-start(f32[320]{0:T(512)} %copy-done.80) | copy-start | bytes 3844
  1684.6 61.9 %copy-start.85 = (f32[384]{0:T(512)S(1)}, f32[384]{0:T(512)}, u32[]{:S(2)}) copy-start(f32[384]{0:T(512)} %get-tuple-element.349) | copy-start | bytes 4612
  1684.6 61.9 %copy-start.102 = (f32[320]{0:T(512)S(1)}, f32[320]{0:T(512)}, u32[]{:S(2)}) copy-start(f32[320]{0:T(512)} %copy-done.101) | copy-start | bytes 3844
  1684.6 61.9 %copy-start.104 = (f32[320]{0:T(512)S(1)}, f32[320]{0:T(512)}, u32[]{:S(2)}) copy-start(f32[320]{0:T(512)} %copy-done.103) | copy-start | bytes 3844
  1684.6 61.9 %copy-start.106 = (f32[320]{0:T(512)S(1)}, f32[320]{0:T(512)}, u32[]{:S(2)}) copy-start(f32[320]{0:T(512)} %copy-done.105) | copy-start | bytes 3844
  1684.6 61.9 %copy-start.108 = (f32[320]{0:T(512)S(1)}, f32[320]{0:T(512)}, u32[]{:S(2)}) copy-start(f32[320]{0:T(512)} %copy-done.107) | copy-start | bytes 3844
  1684.6 61.9 %copy-start.116 = (f32[320]{0:T(512)S(1)}, f32[320]{0:T(512)}, u32[]{:S(2)}) copy-start(f32[320]{0:T(512)} %get-tuple-element.351) | copy-start | bytes 3844
  1684.6 61.9 %copy-start.117 = (f32[320]{0:T(512)S(1)}, f32[320]{0:T(512)}, u32[]{:S(2)}) copy-start(f32[320]{0:T(512)} %get-tuple-element.352) | copy-start | bytes 3844
  (131 other events, 994.6 us)
Sparse Core Ops, SparseCore 0:
  10.3 57.6 all-gather.4
  70.3 38.9 all-gather.6
  322.3 13.8 reduce-scatter.39
  343.1 13.8 reduce-scatter.43
  359.1 42.2 all-gather.8
  403.5 40.9 all-gather.10
  454.9 14.0 reduce-scatter.45
  471.9 15.2 reduce-scatter.41
  542.7 15.2 reduce-scatter.51
  561.6 15.2 reduce-scatter.47
  655.4 15.2 reduce-scatter.49
  719.5 15.2 reduce-scatter.53
  738.9 58.1 reduce-scatter.33
  801.4 67.2 reduce-scatter.31
  873.0 74.4 reduce-scatter.35
  952.2 74.5 reduce-scatter.37
  1550.4 111.3 reduce-scatter.29
where the time goes:
time: 1770 us; the launch traced here: 1760 us
  matrix products  1080 us (61%)
  local copies, waits for them, and re-layouts  320 us (18%)
  blocking collectives  187 us (11%)
  waiting for transfers between devices  111 us (6%)
  other arithmetic  39.1 us (2%)
    conv_general_dilated x2, matrix products, conv_weight_grad(): lax.conv_general_dilated(left_side, right_side, (1,), [(0, 0)], dimension...  496 us
    conv_general_dilated x2, matrix products, conv_input_grad(): lax.conv_general_dilated(grad_low, turned, (1,), [(tap_count // 2 - 1, ta...  260 us
    conv_general_dilated x2, matrix products, conv_forward(): lax.conv_general_dilated(inputs, kernel, (1,), [(tap_count // 2, tap_coun...  166 us
    rev x2, local copies, waits for them, and re-layouts, conv_input_grad(): kernel.reshape(tap_count, group_width, group_count, group_width)  88 us
    unnamed x356, local copies, waits for them, and re-layouts  71.5 us
    psum x1, blocking collectives, body(): lax.psum((gain_sums, bias_sums, up_bias_sum), 'dp')  57.7 us
    unnamed x25, waiting for transfers between devices  38.1 us
    all_gather x1, waiting for transfers between devices, fetch(): lax.all_gather(down_weight, 'dp', axis=1, tiled=True)  35.5 us
  transfers between devices with their start and end apart: 17, of which 6 were waited for; matrix products, arithmetic and copies ran while one was open for 74% of the time, Pallas kernels for 0%

commit v1 on v0

v1 whole, which is shorter than its diff:
```python
from functools import partial

import jax
import jax.numpy as jnp
from jax import lax
from jax.experimental import pallas as pl
from jax.experimental.pallas import tpu as pltpu
from jax.sharding import PartitionSpec as P

D = 768
HEAD_DIM = 64
KERNEL = 128
GROUPS = 16


EPSILON = 1e-05
MASKED = -1e30


def spread_features(features):
    return lax.all_gather(features.astype(jnp.bfloat16), "mp", axis=2, tiled=True)


def spread_grads(features):
    return lax.all_gather(features.astype(jnp.bfloat16), "mp", axis=2, tiled=True)


def fold_partials(features):
    return lax.psum_scatter(
        features.astype(jnp.bfloat16), "mp", scatter_dimension=2, tiled=True
    ).astype(jnp.float32)


def fold_grads(features):
    return lax.psum_scatter(
        features.astype(jnp.bfloat16), "mp", scatter_dimension=2, tiled=True
    ).astype(jnp.float32)


def norm_forward(features, gain_vec, shift_vec):
    row_total = lax.psum(jnp.sum(features, axis=-1), "mp")
    center = features - (row_total / D)[..., None]
    spread = lax.psum(jnp.sum(center * center, axis=-1), "mp")
    variance = spread / D
    inv_scale = lax.rsqrt(variance + EPSILON)[..., None]
    normed = center * inv_scale
    return (normed * gain_vec + shift_vec, normed, inv_scale)


def norm_backward(incoming, normed, inv_scale, gain_vec):
    scaled = incoming * gain_vec
    first_sum, second_sum = lax.psum(
        (jnp.sum(scaled, axis=-1), jnp.sum(scaled * normed, axis=-1)), "mp"
    )
    result = inv_scale * (
        scaled - (first_sum / D)[..., None] - normed * (second_sum / D)[..., None]
    )
    return (result, jnp.sum(incoming * normed, axis=(0, 1)), jnp.sum(incoming, axis=(0, 1)))


def conv_fwd_kernel(x_ref, live_ref, w_ref, bias_ref, conv_ref, xt, ot, x16):
    g = pl.program_id(0)
    R, T, C = x_ref.shape
    L = xt.shape[2]
    nb, gw, na = 8, 48, 16
    @pl.when(g == 0)
    def _():
        for r in range(R):
            m = x_ref[r].astype(jnp.float32) * live_ref[r].astype(jnp.float32)
            m = jnp.concatenate([m, jnp.zeros((L - T, C), jnp.float32)], axis=0)
            xt[r] = m.T
    rows = pl.ds(pl.multiple_of(g * gw, 16), gw)
    for r in range(R):
        xg = xt[r, rows, :]
        for a in range(na):
            sh = (64 - 8 * a) % L
            v = pltpu.roll(xg, sh, axis=1) if sh else xg
            x16[a * gw:(a + 1) * gw, r * L:(r + 1) * L] = v.astype(jnp.bfloat16)
    w = w_ref[...].reshape(na * gw, nb * gw)
    y = lax.dot_general(w, x16[...], (((0,), (0,)), ((), ())), preferred_element_type=jnp.float32)
    for r in range(R):
        acc = y[0:gw, r * L:(r + 1) * L]
        for b in range(1, nb):
            acc = acc + pltpu.roll(y[b * gw:(b + 1) * gw, r * L:(r + 1) * L], L - b, axis=1)
        ot[r, rows, :] = acc
    @pl.when(g == pl.num_programs(0) - 1)
    def _():
        for r in range(R):
            conv_ref[r] = ot[r].T[:T] + bias_ref[...]

def conv_fwd(x, live, w, bias):
    R, T, C = x.shape
    L = 384
    return pl.pallas_call(
        conv_fwd_kernel,
        grid=(8,),
        in_specs=[pl.BlockSpec((R, T, C), lambda g: (0, 0, 0)),
                  pl.BlockSpec((R, T, 1), lambda g: (0, 0, 0)),
                  pl.BlockSpec((16, 1, 48, 384), lambda g: (0, g, 0, 0)),
                  pl.BlockSpec((1, C), lambda g: (0, 0))],
        out_specs=pl.BlockSpec((R, T, C), lambda g: (0, 0, 0)),
        out_shape=jax.ShapeDtypeStruct((R, T, C), jnp.float32),
        scratch_shapes=[pltpu.VMEM((R, C, L), jnp.float32), pltpu.VMEM((R, C, L), jnp.float32), pltpu.VMEM((768, R * L), jnp.bfloat16)],
        compiler_params=pltpu.CompilerParams(vmem_limit_bytes=48 << 20),
        name="conv_fwd",
    )(x, live, w, bias)

def conv_bwd_kernel(x_ref, live_ref, w_ref, gl_ref, gw_ref, gi_ref, xt, gt, ot, x16, g8):
    g = pl.program_id(0)
    R, T, C = x_ref.shape
    L = xt.shape[2]
    nb, gw, na = 8, 48, 16
    @pl.when(g == 0)
    def _():
        for r in range(R):
            m = x_ref[r].astype(jnp.float32) * live_ref[r].astype(jnp.float32)
            z = jnp.zeros((L - T, C), jnp.float32)
            xt[r] = jnp.concatenate([m, z], axis=0).T
            gt[r] = jnp.concatenate([gl_ref[r].astype(jnp.float32), z], axis=0).T
    rows = pl.ds(pl.multiple_of(g * gw, 16), gw)
    for r in range(R):
        xg = xt[r, rows, :]
        for a in range(na):
            sh = (64 - 8 * a) % L
            v = pltpu.roll(xg, sh, axis=1) if sh else xg
            x16[a * gw:(a + 1) * gw, r * L:(r + 1) * L] = v.astype(jnp.bfloat16)
        gg = gt[r, rows, :]
        for b in range(nb):
            v = pltpu.roll(gg, b, axis=1) if b else gg
            g8[b * gw:(b + 1) * gw, r * L:(r + 1) * L] = v.astype(jnp.bfloat16)
    grad = lax.dot_general(x16[...], g8[...], (((1,), (1,)), ((), ())), preferred_element_type=jnp.float32)
    gw_ref[...] = grad.reshape(na, 1, gw, nb * gw).astype(gw_ref.dtype)
    w = w_ref[...].reshape(na * gw, nb * gw)
    z = jnp.dot(w, g8[...], preferred_element_type=jnp.float32)
    for r in range(R):
        acc = None
        for a in range(na):
            sh = (8 * a - 64) % L
            v = z[a * gw:(a + 1) * gw, r * L:(r + 1) * L]
            v = pltpu.roll(v, sh, axis=1) if sh else v
            acc = v if acc is None else acc + v
        ot[r, rows, :] = acc
    @pl.when(g == pl.num_programs(0) - 1)
    def _():
        for r in range(R):
            gi_ref[r] = ot[r].T[:T] * live_ref[r].astype(jnp.float32)

def conv_bwd(x, live, w, gl, gdtype=jnp.float32):
    R, T, C = x.shape
    L = 384
    full = lambda g: (0, 0, 0)
    return pl.pallas_call(
        conv_bwd_kernel,
        grid=(8,),
        in_specs=[pl.BlockSpec((R, T, C), full), pl.BlockSpec((R, T, 1), full),
                  pl.BlockSpec((16, 1, 48, 384), lambda g: (0, g, 0, 0)),
                  pl.BlockSpec((R, T, C), full)],
        out_specs=[pl.BlockSpec((16, 1, 48, 384), lambda g: (0, g, 0, 0)), pl.BlockSpec((R, T, C), full)],
        out_shape=[jax.ShapeDtypeStruct((16, 8, 48, 384), gdtype), jax.ShapeDtypeStruct((R, T, C), jnp.float32)],
        scratch_shapes=[pltpu.VMEM((R, C, L), jnp.float32)] * 3 + [pltpu.VMEM((768, R * L), jnp.bfloat16), pltpu.VMEM((384, R * L), jnp.bfloat16)],
        compiler_params=pltpu.CompilerParams(vmem_limit_bytes=48 << 20),
        name="conv_bwd",
    )(x, live, w, gl)

def taps_in(weight):
    blocks = weight.reshape(-1, 8, 48, 8, 48)
    return blocks.transpose(0, 3, 2, 1, 4).reshape(-1, 8, 48, 384)


def taps_out(grad):
    blocks = grad.reshape(-1, 8, 48, 8, 48)
    return blocks.transpose(0, 3, 2, 1, 4).reshape(-1, 384)


def heads_first(features):
    row_count, frame_count, width = features.shape
    return (
        features.reshape(row_count, frame_count, width // HEAD_DIM, HEAD_DIM)
        .transpose(0, 2, 1, 3)
        .reshape(-1, frame_count, HEAD_DIM)
    )


def heads_last(items, row_count):
    item_count, frame_count, head_width = items.shape
    return (
        items.reshape(row_count, item_count // row_count, frame_count, head_width)
        .transpose(0, 2, 1, 3)
        .reshape(row_count, frame_count, -1)
    )


def masked_scores(queries, keys_low, clip_ids):
    scale_factor = queries.shape[-1] ** (-0.5)
    scores = (
        jnp.einsum("qe,ke->qk", queries, keys_low, preferred_element_type=jnp.float32)
        * scale_factor
    )
    same_clip = clip_ids[:, None] == clip_ids[None, :]
    return jnp.where(same_clip, scores, MASKED)


def attend_one(item_pack):
    queries, keys_low, values, clip_ids = item_pack
    scores = masked_scores(queries, keys_low, clip_ids)
    row_max = jnp.max(scores, axis=-1, keepdims=True)
    weights = jnp.exp(scores - row_max)
    row_total = jnp.sum(weights, axis=-1, keepdims=True)
    probabilities = (weights / row_total).astype(jnp.bfloat16)
    context = jnp.dot(probabilities, values, preferred_element_type=jnp.float32).astype(
        jnp.bfloat16
    )
    return (context, (row_max + jnp.log(row_total))[:, 0])


def attend_back(item_pack):
    queries, keys_low, values, clip_ids, log_total, grad_context = item_pack
    scale_factor = queries.shape[-1] ** (-0.5)
    scores = masked_scores(queries, keys_low, clip_ids)
    probabilities = jnp.exp(scores - log_total[:, None])
    grad_probs = jnp.einsum("qe,ke->qk", grad_context, values, preferred_element_type=jnp.float32)
    row_dot = jnp.sum(grad_probs * probabilities, axis=-1, keepdims=True)
    grad_scores = (probabilities * (grad_probs - row_dot)).astype(jnp.bfloat16)
    grad_queries = (
        jnp.dot(grad_scores, keys_low, preferred_element_type=jnp.float32) * scale_factor
    ).astype(jnp.bfloat16)
    grad_keys = (
        jnp.einsum("qk,qe->ke", grad_scores, queries, preferred_element_type=jnp.float32)
        * scale_factor
    ).astype(jnp.bfloat16)
    grad_values = jnp.einsum(
        "qk,qe->ke",
        probabilities.astype(jnp.bfloat16),
        grad_context,
        preferred_element_type=jnp.float32,
    ).astype(jnp.bfloat16)
    return (grad_queries, grad_keys, grad_values)


def body(
    frames,
    segment_ids,
    live,
    conv_weight,
    qkv_weight,
    out_weight,
    up_weight,
    down_weight,
    up_bias,
    gains,
    biases,
    out_grad,
):
    row_count = frames.shape[0]
    width = frames.shape[2]
    head_count = width // HEAD_DIM
    hid = up_weight.shape[1]
    gelu_exact = partial(jax.nn.gelu, approximate=False)
    whole_blocks = conv_weight.shape[0] % (8 * 48) == 0
    if whole_blocks:
        conv_full = lax.all_gather(taps_in(conv_weight), "dp", axis=0, tiled=True)
    else:
        conv_full = taps_in(lax.all_gather(conv_weight, "dp", axis=0, tiled=True))
    wall = jnp.concatenate(
        [qkv_weight.reshape(-1, 3 * width), out_weight.T, up_weight, down_weight.T], axis=1
    )
    wall = lax.all_gather(wall, "dp", axis=0, tiled=True)
    cuts = (3 * width, 4 * width, 4 * width + hid)
    qkv_full, out_t, up_full, down_t = jnp.split(wall, cuts, axis=1)
    alive = live[..., None]
    conv_out = conv_fwd(frames, alive, conv_full, biases[0:1])
    positioned = frames.astype(jnp.float32) + gelu_exact(conv_out)
    first_norm, normed_zero, scale_zero = norm_forward(positioned, gains[0], biases[1])
    first_full = spread_features(first_norm)
    projected = jnp.einsum("rsd,dn->rsn", first_full, qkv_full, preferred_element_type=jnp.float32)
    query_items = heads_first((projected[:, :, :width] + biases[2]).astype(jnp.bfloat16))
    key_items = heads_first(projected[:, :, width : 2 * width].astype(jnp.bfloat16))
    value_items = heads_first((projected[:, :, 2 * width :] + biases[3]).astype(jnp.bfloat16))
    item_ids = jnp.repeat(segment_ids, head_count, axis=0)
    context_items, log_total = jax.vmap(lambda *p: attend_one(p))(
        query_items, key_items, value_items, item_ids
    )
    context = heads_last(context_items, row_count)
    attended = fold_partials(
        jnp.einsum("rsh,dh->rsd", context, out_t, preferred_element_type=jnp.float32)
    )
    second_norm, normed_one, scale_one = norm_forward(
        first_norm + attended + biases[4], gains[1], biases[5]
    )
    second_full = spread_features(second_norm)
    up_proj = (
        jnp.einsum("rsd,df->rsf", second_full, up_full, preferred_element_type=jnp.float32)
        + up_bias
    )
    hidden = gelu_exact(up_proj).astype(jnp.bfloat16)
    down_proj = fold_partials(
        jnp.einsum("rsf,df->rsd", hidden, down_t, preferred_element_type=jnp.float32)
    )
    mixed_out, normed_two, scale_two = norm_forward(
        second_norm + down_proj + biases[6], gains[2], biases[7]
    )
    incoming = out_grad.astype(jnp.float32)
    grad_second, gain_two, shift_two = norm_backward(incoming, normed_two, scale_two, gains[2])
    grad_down_full = spread_grads(grad_second)
    grad_down = jnp.einsum(
        "rsf,rsd->df", hidden, grad_down_full, preferred_element_type=jnp.float32
    )
    grad_hidden = jnp.einsum(
        "rsd,df->rsf", grad_down_full, down_t, preferred_element_type=jnp.float32
    )
    up_pull = jax.vjp(gelu_exact, up_proj)[1]
    grad_up_low = up_pull(grad_hidden)[0].astype(jnp.bfloat16)
    grad_up = jnp.einsum("rsd,rsf->df", second_full, grad_up_low, preferred_element_type=jnp.float32)
    grad_up_bias = jnp.sum(grad_up_low, axis=(0, 1), dtype=jnp.float32)
    grad_h_one = grad_second + fold_grads(
        jnp.einsum("rsf,df->rsd", grad_up_low, up_full, preferred_element_type=jnp.float32)
    )
    grad_first, gain_one, shift_one = norm_backward(grad_h_one, normed_one, scale_one, gains[1])
    grad_att_full = spread_grads(grad_first)
    grad_out = jnp.einsum(
        "rsh,rsd->dh", context, grad_att_full, preferred_element_type=jnp.float32
    )
    grad_context = jnp.einsum(
        "rsd,dh->rsh", grad_att_full, out_t, preferred_element_type=jnp.float32
    ).astype(jnp.bfloat16)
    grad_query_items, grad_key_items, grad_value_items = jax.vmap(lambda *p: attend_back(p))(
        query_items, key_items, value_items, item_ids, log_total, heads_first(grad_context)
    )
    grad_queries = heads_last(grad_query_items, row_count)
    grad_values = heads_last(grad_value_items, row_count)
    grad_stack = jnp.concatenate(
        [grad_queries, heads_last(grad_key_items, row_count), grad_values], axis=2
    )
    grad_qkv = jnp.einsum(
        "rsd,rsn->dn", first_full, grad_stack, preferred_element_type=jnp.float32
    )
    grad_h_zero = grad_first + fold_grads(
        jnp.einsum("rsn,dn->rsd", grad_stack, qkv_full, preferred_element_type=jnp.float32)
    )
    grad_pos, gain_zero, shift_zero = norm_backward(grad_h_zero, normed_zero, scale_zero, gains[0])
    conv_pull = jax.vjp(gelu_exact, conv_out)[1]
    grad_conv_low = conv_pull(grad_pos)[0].astype(jnp.bfloat16)
    grad_conv, grad_in = conv_bwd(frames, alive, conv_full, grad_conv_low, jnp.bfloat16)
    grad_wall = jnp.concatenate([grad_qkv, grad_out, grad_up, grad_down], axis=1)
    grad_wall = lax.psum_scatter(
        grad_wall.astype(jnp.bfloat16), "dp", scatter_dimension=0, tiled=True
    ).astype(jnp.float32)
    qkv_part, out_part, up_part, down_part = jnp.split(grad_wall, cuts, axis=1)
    if whole_blocks:
        conv_part = taps_out(
            lax.psum_scatter(grad_conv, "dp", scatter_dimension=0, tiled=True).astype(jnp.float32)
        )
    else:
        conv_part = lax.psum_scatter(
            taps_out(grad_conv), "dp", scatter_dimension=0, tiled=True
        ).astype(jnp.float32)
    gain_terms = jnp.stack([gain_zero, gain_one, gain_two])
    bias_terms = jnp.stack(
        [
            jnp.sum(grad_conv_low, axis=(0, 1), dtype=jnp.float32),
            shift_zero,
            jnp.sum(grad_queries, axis=(0, 1), dtype=jnp.float32),
            jnp.sum(grad_values, axis=(0, 1), dtype=jnp.float32),
            jnp.sum(grad_first, axis=(0, 1)),
            shift_one,
            jnp.sum(grad_second, axis=(0, 1)),
            shift_two,
        ]
    )
    gain_total, bias_total, up_bias_total = lax.psum((gain_terms, bias_terms, grad_up_bias), "dp")
    return (
        mixed_out.astype(jnp.bfloat16),
        grad_pos + grad_in,
        conv_part,
        qkv_part.reshape(-1, 3, width),
        out_part.T,
        up_part,
        down_part.T,
        up_bias_total,
        gain_total,
        bias_total,
    )


def solution(mesh):
    placed = (
        P("dp", None, "mp"),
        P("dp", None),
        P("dp", None),
        P("dp", "mp"),
        P("dp", None, "mp"),
        P("mp", "dp"),
        P("dp", "mp"),
        P("mp", "dp"),
        P("mp"),
        P(None, "mp"),
        P(None, "mp"),
        P("dp", None, "mp"),
    )
    return jax.shard_map(
        body,
        mesh=mesh,
        in_specs=placed,
        out_specs=(
            P("dp", None, "mp"),
            P("dp", None, "mp"),
            P("dp", "mp"),
            P("dp", None, "mp"),
            P("mp", "dp"),
            P("dp", "mp"),
            P("mp", "dp"),
            P("mp"),
            P(None, "mp"),
            P(None, "mp"),
        ),
        check_vma=False,
    )
```

time: 1770 us -> 645 us (0.36)
  matrix products: 1080 us -> 62.1 us
  local copies, waits for them, and re-layouts: 320 us -> 86.1 us
  waiting for transfers between devices: 111 us -> 242 us
  blocking collectives: 187 us -> 154 us
  Pallas kernels: 0 us -> 28.6 us
    conv_general_dilated x6 -> x0, matrix products: 922 us -> none  [the longest x2 496 us: conv_weight_grad(): lax.conv_general_dilated(left_side, right_side, (1,), [(0, 0)], dimension...]
    rev x2 -> x0, local copies, waits for them, and re-layouts: 88 us -> none  [conv_input_grad(): kernel.reshape(tap_count, group_width, group_count, group_width)]
    reduce_scatter x5 -> x2, waiting for transfers between devices: 0.02 us -> 79.1 us  [the longest x1 79.1 us: body(): lax.psum_scatter(grad_wall.astype(jnp.bfloat16), 'dp', scatter_dimension=...]
    unnamed x25 -> x12, waiting for transfers between devices: 38.1 us -> 77.4 us
    transpose x8 -> x2, local copies, waits for them, and re-layouts: 33.6 us -> 1.37 us  [body(): return (mixed_out.astype(jnp.bfloat16), grad_pos + grad_in, conv_part, qk...]
    add x16 -> x0, local copies, waits for them, and re-layouts: 31.6 us -> none  [the longest x2 30.2 us: body(): running + addend]
    pallas_call x0 -> x2, Pallas kernels: none -> 28.6 us  [the longest x1 17.9 us: conv_bwd(): pl.pallas_call(conv_bwd_kernel, grid=(8,), in_specs=[pl.BlockSpec((R, T,...]
    all_gather x1 -> x0, blocking collectives: 27 us -> none  [fetch(): lax.all_gather(out_weight, 'dp', axis=1, tiled=True)]
  transfers between devices with their start and end apart: 17 -> 8, of which waited for: 6 -> 7; matrix products, arithmetic and copies ran while one was open for 74% -> 5% of each run, Pallas kernels for 0% -> 2%
where the time goes in v1:
time: 645 us; the launch traced here: 637 us
  waiting for transfers between devices  242 us (38%)
  blocking collectives  154 us (24%)
  local copies, waits for them, and re-layouts  86.1 us (13%)
  matrix products  62.1 us (10%)
  other arithmetic  48.5 us (8%)
  Pallas kernels  28.6 us (4%)
  between operations  15 us (2%)
    reduce_scatter x1, waiting for transfers between devices, body(): lax.psum_scatter(grad_wall.astype(jnp.bfloat16), 'dp', scatter_dimension=...  79.1 us
    unnamed x12, waiting for transfers between devices  77.4 us
    psum x1, blocking collectives, body(): lax.psum((gain_terms, bias_terms, grad_up_bias), 'dp')  61.5 us
    unnamed x86, local copies, waits for them, and re-layouts  58.2 us
    all_gather x1, waiting for transfers between devices, body(): conv_full = lax.all_gather(taps_in(conv_weight), 'dp', axis=0, tiled=True)  55 us
    all_gather x1, waiting for transfers between devices, body(): wall = lax.all_gather(wall, 'dp', axis=0, tiled=True)  30.6 us
    all_gather x2, blocking collectives, spread_features(): lax.all_gather(features.astype(jnp.bfloat16), 'mp', axis=2, tiled=True)  24.7 us
    all_gather x2, blocking collectives, spread_grads(): lax.all_gather(features.astype(jnp.bfloat16), 'mp', axis=2, tiled=True)  23.1 us
  transfers between devices with their start and end apart: 8, of which 7 were waited for; matrix products, arithmetic and copies ran while one was open for 5% of the time, Pallas kernels for 2%

profile of v1, /device:TPU:0, one launch (start us, length us, event | category | flops | bytes accessed | tf_op | source)
XLA Modules:
  0.0 637.0 jit_solution(3501596823722379152)
XLA Ops:
  12.4 55.0 %all-gather.3.cloned.1.call-done.w_ref = bf16[16,8,48,384]{3,2,1,0:T(8,128)(2,1)} async-done(((bf16[1,8,48,384]{3,2,1,0:T(8,128)(2,1)}), bf16[16,8,48,384]{3,2,1,0:T(8,128)(2,1)}) %all-gather.3.cloned.1.call-update) | async-done | bytes 4718608 | tf_op jit(solution)/shard_map/all_gather | solution.py:261
  67.3 10.7 %conv_fwd.1 = f32[2,320,384]{2,1,0:T(8,128)S(1)} custom-call(bf16[2,320,384]{2,1,0:T(8,128)(2,1)S(1)} %copy-done, s32[2,320,1]{2,1,0:T(8,128)S(1)} %copy.60.live_ref, bf16[16,8,48,384]{3,2,1,0:T(8,128)(2,1)} %all-gather.3.cloned.1.call-done.w_ref, f32[1,384]{1,0:T(1,128)S(1)} %get-tuple-element.97.bias_ref), custom_call_target="tpu_custom_call" | custom-call | tf_op jit(solution)/shard_map/conv_fwd/pallas_call | solution.py:94
  78.0 3.1 fusion.55
  81.2 4.9 psum.105
  86.4 4.9 psum.106
  91.6 13.2 %all_gather.19 = bf16[2,320,768]{2,1,0:T(8,128)(2,1)} all-gather(bf16[2,320,384]{2,1,0:T(8,128)(2,1)S(1)} %fusion.43), channel_id=1, replica_groups=mesh['dp'=16,'mp'=2] {'mp'}, dimensions={2}, use_global_device_ids=true | all-gather | bytes 1474560 | tf_op jit(solution)/shard_map/all_gather | solution.py:21
  104.8 30.6 %all-gather.5.cloned.1.call-done = bf16[768,4608]{1,0:T(8,128)(2,1)} async-done(((bf16[48,4608]{1,0:T(8,128)(2,1)}), bf16[768,4608]{1,0:T(8,128)(2,1)}) %all-gather.5.cloned.1.call-update) | async-done | bytes 7077904 | tf_op jit(solution)/shard_map/all_gather | solution.py:267
  135.4 3.2 fusion.21
  144.4 2.8 fusion.57
  153.3 4.7 copy.85
  158.0 3.6 reshape.166
  161.6 18.2 %reduce-scatter.19.cloned.1.call-done = bf16[384,640]{1,0:T(8,128)(2,1)} async-done(((bf16[768,640]{1,0:T(8,128)(2,1)}), bf16[384,640]{1,0:T(8,128)(2,1)}) %reduce-scatter.19.cloned.1.call-update) | async-done | bytes 491536
  186.0 4.9 psum.107
  192.4 4.9 psum.108
  198.8 11.5 %all_gather.21 = bf16[2,320,768]{2,1,0:T(8,128)(2,1)S(1)} all-gather(bf16[2,320,384]{2,1,0:T(8,128)(2,1)S(1)} %fusion.44), channel_id=1, replica_groups=mesh['dp'=16,'mp'=2] {'mp'}, dimensions={2}, use_global_device_ids=true | all-gather | bytes 1474560 | tf_op jit(solution)/shard_map/all_gather | solution.py:21
  210.3 4.7 fusion.42
  215.1 10.1 %multiply_convert_fusion.1 = (bf16[2,320,1536]{2,1,0:T(8,128)(2,1)S(1)}, f32[2,320,1536]{2,1,0:T(8,128)}) fusion(f32[2,320,1536]{2,1,0:T(8,128)S(1)} %get-tuple-element.100, f32[1536]{0:T(1024)S(1)} %copy-done.27, u8[320,1536]{1,0:T(8,128)(4,1)S(1)} %get-tuple-element.45, u8[320,1536]{1,0:T(8,128)(4,1)S(1)} %get-tuple-element.44), kind=kLoop, calls=%fused_computation.20 | loop fusion | flops 69795840 | bytes 10819584 | tf_op jit(solution)/shard_map/convert_element_type | solution.py:295
  226.4 4.4 fusion.16
  230.8 4.7 copy.87
  235.5 3.6 reshape.168
  239.1 19.7 %reduce-scatter.21.cloned.1.call-done = bf16[384,640]{1,0:T(8,128)(2,1)} async-done(((bf16[768,640]{1,0:T(8,128)(2,1)}), bf16[384,640]{1,0:T(8,128)(2,1)}) %reduce-scatter.21.cloned.1.call-update) | async-done | bytes 491536
  265.4 4.9 psum.109
  271.8 4.9 psum.110
  278.7 5.0 all-reduce.3
  283.7 2.9 fusion.50
  286.6 10.4 %all_gather.22 = bf16[2,320,768]{2,1,0:T(8,128)(2,1)S(1)} all-gather(bf16[2,320,384]{2,1,0:T(8,128)(2,1)S(1)} %get-tuple-element.83), channel_id=1, replica_groups=mesh['dp'=16,'mp'=2] {'mp'}, dimensions={2}, use_global_device_ids=true | all-gather | bytes 1474560 | tf_op jit(solution)/shard_map/all_gather | solution.py:25
  297.0 5.6 convert_reduce_fusion
  304.0 4.3 fusion.17
  308.3 4.7 copy.89
  313.0 3.6 reshape.170
  316.6 19.7 %reduce-scatter.23.cloned.1.call-done = bf16[384,640]{1,0:T(8,128)(2,1)} async-done(((bf16[768,640]{1,0:T(8,128)(2,1)}), bf16[384,640]{1,0:T(8,128)(2,1)}) %reduce-scatter.23.cloned.1.call-update) | async-done | bytes 491536
  343.5 5.0 all-reduce.2
  351.5 12.7 %all_gather.23 = bf16[2,320,768]{2,1,0:T(8,128)(2,1)S(1)} all-gather(bf16[2,320,384]{2,1,0:T(8,128)(2,1)S(1)} %convert_element_type.122), channel_id=1, replica_groups=mesh['dp'=16,'mp'=2] {'mp'}, dimensions={2}, use_global_device_ids=true | all-gather | bytes 1474560 | tf_op jit(solution)/shard_map/all_gather | solution.py:25
  369.0 4.7 fusion.26
  373.8 4.2 multiply_reduce_fusion
  387.9 4.4 convolution_convert_fusion
  392.3 4.7 copy.91
  397.0 3.6 reshape.172
  400.7 19.7 %reduce-scatter.25.cloned.1.call-done = bf16[384,640]{1,0:T(8,128)(2,1)} async-done(((bf16[768,640]{1,0:T(8,128)(2,1)}), bf16[384,640]{1,0:T(8,128)(2,1)}) %reduce-scatter.25.cloned.1.call-update) | async-done | bytes 491536
  423.2 2.9 copy.92
  428.8 5.4 all-reduce.1
  436.4 17.9 %conv_bwd.1 = (bf16[16,8,48,384]{3,2,1,0:T(8,128)(2,1)}, f32[2,320,384]{2,1,0:T(8,128)S(1)}) custom-call(bf16[2,320,384]{2,1,0:T(8,128)(2,1)S(1)} %copy-done, s32[2,320,1]{2,1,0:T(8,128)S(1)} %copy.60.live_ref, bf16[16,8,48,384]{3,2,1,0:T(8,128)(2,1)} %all-gather.3.cloned.1.call-done.w_ref, bf16[2,320,384]{2,1,0:T(8,128)(2,1)S(1)} %get-tuple-element.81.gl_ref), custom_call_target="tpu_custom_call" | custom-call | tf_op jit(solution)/shard_map/conv_bwd/pallas_call | solution.py:152
  454.4 5.4 bitcast_convert_fusion
  459.9 3.4 bitcast_convert_fusion.1
  466.2 3.6 fusion.8
  469.8 3.3 pad_maximum_fusion
  474.6 61.5 %all-reduce = (f32[1536]{0:T(1024)}, f32[3,384]{1,0:T(4,128)}, f32[8,384]{1,0:T(8,128)}) all-reduce(f32[1536]{0:T(1024)S(1)} %get-tuple-element.103, f32[3,384]{1,0:T(4,128)S(1)} %pad_maximum_fusion.5, f32[8,384]{1,0:T(8,128)S(1)} %stack.51), channel_id=1, replica_groups=mesh['dp'=16,'mp'=2] {'dp'}, use_global_device_ids=true, to_apply=%region_34.35 | all-reduce | flops 5760 | bytes 46080 | tf_op jit(solution)/shard_map/psum | solution.py:370
  545.2 79.1 %reduce-scatter.17.cloned.1.call-done = bf16[48,4608]{1,0:T(8,128)(2,1)} async-done(((bf16[768,4608]{1,0:T(8,128)(2,1)}), bf16[48,4608]{1,0:T(8,128)(2,1)}) %reduce-scatter.17.cloned.1.call-update) | async-done | bytes 442384 | tf_op jit(solution)/shard_map/reduce_scatter | solution.py:345
  (173 shorter events, 90.9 us)
Async XLA Ops:
  7.2 4.0 copy-start.24
  7.2 4.0 copy-start.22
  7.2 4.0 copy-start.23
  7.2 4.0 copy-start.25
  7.2 4.8 copy-start.30
  7.2 4.9 copy-start.29
  7.2 5.0 copy-start.28
  7.2 5.1 copy-start.26
  7.3 60.1 %copy-start = (bf16[2,320,384]{2,1,0:T(8,128)(2,1)S(1)}, bf16[2,320,384]{2,1,0:T(8,128)(2,1)}, u32[]{:S(2)}) copy-start(bf16[2,320,384]{2,1,0:T(8,128)(2,1)} %x_ref.3) | copy-start | bytes 1474564
  7.3 60.1 %all-gather.3.cloned.1.call-start = ((), (), s32[]{:S(2)}) async-start(), calls=%async_computation.6 | async-start | bytes 5013504 | tf_op jit(solution)/shard_map/all_gather | solution.py:261
  11.1 124.3 %all-gather.5.cloned.1.call-start = ((), (), s32[]{:S(2)}) async-start(), calls=%async_computation.7 | async-start | bytes 7520256 | tf_op jit(solution)/shard_map/all_gather | solution.py:267
  12.0 167.8 %reduce-scatter.19.cloned.1.call-start = ((), (), s32[]{:S(2)}) async-start(), calls=%async_computation.10 | async-start | bytes 1474560
  144.3 3.7 copy-start.7
  147.2 2.5 copy-start.1
  149.6 0.9 copy-start.20
  161.6 97.3 %reduce-scatter.21.cloned.1.call-start = ((), (), s32[]{:S(2)}) async-start(), calls=%async_computation.11 | async-start | bytes 1474560
  181.9 28.4 %copy-start.27 = (f32[1536]{0:T(1024)S(1)}, f32[1536]{0:T(1024)}, u32[]{:S(2)}) copy-start(f32[1536]{0:T(1024)} %param.20) | copy-start | bytes 18436
  210.3 4.7 copy-start.15
  215.0 10.1 %copy-start.5 = (f32[2,320,1536]{2,1,0:T(8,128)}, f32[2,320,1536]{2,1,0:T(8,128)S(1)}, u32[]{:S(2)}) copy-start(f32[2,320,1536]{2,1,0:T(8,128)S(1)} %get-tuple-element.100) | copy-start | bytes 11796484
  225.1 1.3 copy-start.13
  239.1 97.3 %reduce-scatter.23.cloned.1.call-start = ((), (), s32[]{:S(2)}) async-start(), calls=%async_computation.12 | async-start | bytes 1474560
  262.7 21.0 %copy-start.14 = (bf16[2,320,384]{2,1,0:T(8,128)(2,1)S(1)}, bf16[2,320,384]{2,1,0:T(8,128)(2,1)}, u32[]{:S(2)}) copy-start(bf16[2,320,384]{2,1,0:T(8,128)(2,1)} %param.23) | copy-start | bytes 1474564
  283.7 13.3 %copy-start.6 = (f32[2,320,1536]{2,1,0:T(8,128)S(1)}, f32[2,320,1536]{2,1,0:T(8,128)}, u32[]{:S(2)}) copy-start(f32[2,320,1536]{2,1,0:T(8,128)} %copy-done.5) | copy-start | bytes 11796484
  297.0 5.6 copy-start.17
  302.6 1.3 copy-start.31
  316.6 103.8 %reduce-scatter.25.cloned.1.call-start = ((), (), s32[]{:S(2)}) async-start(), calls=%async_computation.13 | async-start | bytes 1474560
  350.4 1.0 copy-start.2
  364.2 0.9 copy-start.18
  369.0 4.8 copy-start.8
  369.0 8.9 %slice-start = ((s8[5898240]{0:T(1024)(128)(4,1)}), s8[4194304]{0:T(1024)(128)(4,1)S(1)}, s32[]{:S(2)}) async-start(s8[5898240]{0:T(1024)(128)(4,1)} %bitcast.131), calls=%async_computation.14 | async-start | bytes 8388608
  373.8 4.2 slice-start.1
  378.0 1.3 copy-start.12
  379.3 1.5 copy-start.11
  379.3 3.4 copy-start.3
  400.6 138.1 %reduce-scatter.15.cloned.1.call-start = ((), (), s32[]{:S(2)}) async-start(), calls=%async_computation.8 | async-start | bytes 5013504 | tf_op jit(solution)/shard_map/reduce_scatter | solution.py:351
  454.4 169.9 %reduce-scatter.17.cloned.1.call-start = ((), (), s32[]{:S(2)}) async-start(), calls=%async_computation.9 | async-start | bytes 7520256 | tf_op jit(solution)/shard_map/reduce_scatter | solution.py:345
  454.4 5.5 copy-start.16
  454.4 5.4 copy-start.32
  459.9 3.4 copy-start.19
  459.9 3.4 copy-start.21
  466.2 3.6 copy-start.9
  466.2 3.6 copy-start.10
  473.2 1.1 copy-start.4
Sparse Core Ops, SparseCore 0:
  11.2 56.0 all-gather.2
  70.2 65.1 all-gather.4
  161.7 18.0 reduce-scatter.18
  239.2 19.5 reduce-scatter.20
  316.7 19.6 reduce-scatter.22
  400.7 19.6 reduce-scatter.24
  454.5 76.1 reduce-scatter.14
  535.2 89.0 reduce-scatter.16

commit v2 on v0

v2 whole, which is shorter than its diff:
```python
import functools

import jax
import jax.numpy as jnp
from jax import lax
from jax.experimental import pallas as pl
from jax.experimental.pallas import tpu as pltpu
from jax.sharding import PartitionSpec as P

MESH = pl.DeviceIdType.MESH
F32, BF16 = jnp.float32, jnp.bfloat16
D, H, FF, HD = 768, 384, 1536, 64
R, T, L = 2, 320, 384
NB, GW, NA = 8, 48, 16
TM = 64
EPS = 1e-5
QKV, OUT, UP, DOWN = 0, 1152, 1536, 3072
NN = (((1,), (0,)), ((), ()))
NT = (((1,), (1,)), ((), ()))
TN = (((0,), (0,)), ((), ()))

def mm(a, b, dims=NN):
    return lax.dot_general(a, b, dims, preferred_element_type=F32)

def gelu_both(v):
    p = 0.5 + 0.5 * lax.erf(v * 0.7071067811865476)
    return v * p, p + v * (0.3989422804014327 * jnp.exp(-0.5 * v * v))

def tiles(body, count=T // TM, init=0):
    return lax.fori_loop(0, count, body, init)

def at(i, size=TM):
    return pl.ds(pl.multiple_of(i * size, size), size)

class Mid:
    def shift_inputs(self, g):
        rows = at(g, GW)
        for r in range(R):
            xg = self.xt[r, rows, :]
            for a in range(NA):
                sh = (64 - 8 * a) % L
                v = pltpu.roll(xg, sh, axis=1) if sh else xg
                self.x16[a * GW:(a + 1) * GW, r * L:(r + 1) * L] = v.astype(BF16)

    def turn_in(self, dst, r, rows):
        dst[r] = jnp.concatenate([rows, jnp.zeros((L - T, H), F32)], axis=0).T

    def conv_forward(self):
        for r in range(R):
            self.turn_in(self.xt, r, self.act[0, r, :, self.own].astype(F32) * self.live[r].astype(F32))

        def group(g, c):
            self.shift_inputs(g)
            w = self.convw[:, at(g, GW), :].reshape(NA * GW, NB * GW)
            y = mm(w, self.x16[...], TN)
            for r in range(R):
                acc = y[0:GW, r * L:(r + 1) * L]
                for b in range(1, NB):
                    acc = acc + pltpu.roll(y[b * GW:(b + 1) * GW, r * L:(r + 1) * L], L - b, axis=1)
                self.ot[r, at(g, GW), :] = acc
            return c
        tiles(group, 8)

    def conv_finish(self, r):
        v = self.ot[r].T[:T] + self.par[3:4, self.own]
        gel, dg = gelu_both(v)
        self.dconv[r] = dg
        self.gc[r, :, self.own] = gel.astype(BF16)

    def norm_first(self, r):
        def tile(i, c):
            v = self.act[0, r, at(i), :].astype(F32) + self.gc[r, at(i), :].astype(F32)
            cen = v - jnp.sum(v, axis=1, keepdims=True) * (1.0 / D)
            inv = lax.rsqrt(jnp.sum(cen * cen, axis=1, keepdims=True) * (1.0 / D) + EPS)
            xh = cen * inv
            n = xh * self.par[0:1, :] + self.par[4:5, :]
            self.xh0[r, at(i), :] = xh
            self.inv0[r, at(i), :] = inv
            self.fn[r, at(i), :] = n
            self.flow[r, at(i), :] = n.astype(BF16)
            return c
        tiles(tile)

    def wall_cols(self, start, size):
        return self.wall[:, :, pl.ds(start, size)].reshape(D, size)

    def wall_rows(self, n, start, size):
        return self.wall[pl.ds(n * 8, 8), :, start:start + size].reshape(H, size)

    def project(self, r):
        for c in range(3):
            v = mm(self.flow[r], self.wall_cols(QKV + c * H, H))
            if c != 1:
                v = v + self.par[5 + c // 2:6 + c // 2, self.own]
            self.qkv[r, :, c * H:(c + 1) * H] = v.astype(BF16)

    def lane_masks(self):
        lane = lax.broadcasted_iota(jnp.int32, (1, 128), 1)
        return [(lane < HD).astype(F32).astype(BF16), (lane >= HD).astype(F32).astype(BF16)]

    def pair(self, ref, r, p, c=0):
        return ref[r, :, pl.ds(pl.multiple_of(p * 128 + c * H, 128), 128)]

    def attend(self, r):
        masks = self.lane_masks()
        same = self.segq[r] == self.segk[r]

        def step(p, c):
            q, k, v = (self.pair(self.qkv, r, p, i) for i in range(3))
            acc = None
            for h in range(2):
                s = mm(q * masks[h], k, NT) * 0.125
                s = jnp.where(same, s, -1e30)
                w = jnp.exp(s - jnp.max(s, axis=1, keepdims=True))
                pr = (w * (1.0 / jnp.sum(w, axis=1, keepdims=True))).astype(BF16)
                self.prob[r * 6 + p * 2 + h] = pr
                o = mm(pr, v * masks[h])
                acc = o if acc is None else acc + o
            self.ctx[r, :, pl.ds(pl.multiple_of(p * 128, 128), 128)] = acc.astype(BF16)
            return c
        tiles(step, 3)
        for n in range(2):
            self.a_own[r, :, n * H:(n + 1) * H] = mm(self.ctx[r], self.wall_rows(n, OUT, H), NT).astype(BF16)

    def norm_second(self, r):
        def tile(i, c):
            v = self.fn[r, at(i), :] + (self.a_own[r, at(i), :].astype(F32) + self.a_peer[r, at(i), :].astype(F32)) + self.par[7:8, :]
            cen = v - jnp.sum(v, axis=1, keepdims=True) * (1.0 / D)
            inv = lax.rsqrt(jnp.sum(cen * cen, axis=1, keepdims=True) * (1.0 / D) + EPS)
            xh = cen * inv
            n = xh * self.par[1:2, :] + self.par[8:9, :]
            self.xh1[r, at(i), :] = xh
            self.inv1[r, at(i), :] = inv
            self.sn[r, at(i), :] = n
            self.slow[r, at(i), :] = n.astype(BF16)
            return c
        tiles(tile)

    def feed_forward(self, r):
        for n in range(4):
            u = mm(self.slow[r], self.wall_cols(UP + n * H, H)) + self.upb[:, n * H:(n + 1) * H]
            gel, dg = gelu_both(u)
            self.hid[r, :, n * H:(n + 1) * H] = gel.astype(BF16)
            self.dg[r, :, n * H:(n + 1) * H] = dg.astype(BF16)
        for n in range(2):
            self.b_own[r, :, n * H:(n + 1) * H] = mm(self.hid[r], self.wall_rows(n, DOWN, FF), NT).astype(BF16)

    def add_sums(self, row, value):
        self.psum[row:row + 1, :] += value

    def norm_third(self, r):
        def tile(i, c):
            v = self.sn[r, at(i), :] + (self.b_own[r, at(i), :].astype(F32) + self.b_peer[r, at(i), :].astype(F32)) + self.par[9:10, :]
            cen = v - jnp.sum(v, axis=1, keepdims=True) * (1.0 / D)
            inv = lax.rsqrt(jnp.sum(cen * cen, axis=1, keepdims=True) * (1.0 / D) + EPS)
            xh = cen * inv
            self.mixf[at(i), :] = (xh * self.par[2:3, :] + self.par[10:11, :]).astype(BF16)
            e = self.act[1, r, at(i), :].astype(F32)
            sc = e * self.par[2:3, :]
            ex = e * xh
            m1 = jnp.sum(sc, axis=1, keepdims=True) * (1.0 / D)
            m2 = jnp.sum(sc * xh, axis=1, keepdims=True) * (1.0 / D)
            g = inv * (sc - m1 - xh * m2)
            self.sn[r, at(i), :] = g
            self.gdl[r, at(i), :] = g.astype(BF16)
            sums = [jnp.sum(w, axis=0, keepdims=True) for w in (ex, e, g)]
            return tuple(x + y for x, y in zip(c, sums))
        z = jnp.zeros((1, D), F32)
        s = tiles(tile, init=(z, z, z))
        for row, val in zip((2, 10, 9), s):
            self.add_sums(row, val)
        self.mixed[r] = self.mixf[:, self.own]

    def feed_backward(self, r):
        for n in range(4):
            gh = mm(self.gdl[r], self.wall_cols(DOWN + n * H, H))
            g = (gh * self.dg[r, :, n * H:(n + 1) * H].astype(F32)).astype(BF16)
            self.dg[r, :, n * H:(n + 1) * H] = g
            self.pout[12 + n:13 + n, :] += jnp.sum(g.astype(F32), axis=0, keepdims=True)
        for n in range(2):
            self.a_own[r, :, n * H:(n + 1) * H] = mm(self.dg[r], self.wall_rows(n, UP, FF), NT).astype(BF16)

    def weight_grad(self, src, other, count, start):
        for n in range(count):
            o = other[:, :, n * H:(n + 1) * H].reshape(R * T, H)
            g = mm(src[...].reshape(R * T, D), o, TN)
            self.wall[:, :, start + n * H:start + (n + 1) * H] = g.reshape(16, 48, H).astype(BF16)

    def norm_second_back(self, r):
        def tile(i, c):
            e = self.sn[r, at(i), :] + (self.a_own[r, at(i), :].astype(F32) + self.a_peer[r, at(i), :].astype(F32))
            xh = self.xh1[r, at(i), :]
            sc = e * self.par[1:2, :]
            m1 = jnp.sum(sc, axis=1, keepdims=True) * (1.0 / D)
            m2 = jnp.sum(sc * xh, axis=1, keepdims=True) * (1.0 / D)
            g = self.inv1[r, at(i), :] * (sc - m1 - xh * m2)
            self.sn[r, at(i), :] = g
            self.gal[r, at(i), :] = g.astype(BF16)
            sums = [jnp.sum(w, axis=0, keepdims=True) for w in (e * xh, e, g)]
            return tuple(x + y for x, y in zip(c, sums))
        z = jnp.zeros((1, D), F32)
        s = tiles(tile, init=(z, z, z))
        for row, val in zip((1, 8, 7), s):
            self.add_sums(row, val)

    def attend_back(self, r):
        self.gctx[r] = mm(self.gal[r], self.wall_cols(OUT, H)).astype(BF16)
        masks = self.lane_masks()

        def step(p, c):
            q, k, v = (self.pair(self.qkv, r, p, i) for i in range(3))
            go = self.pair(self.gctx, r, p)
            gq = gk = gv = None
            for h in range(2):
                gom = go * masks[h]
                gp = mm(gom, v, NT)
                pr = self.prob[r * 6 + p * 2 + h]
                pf = pr.astype(F32)
                gs = (pf * (gp - jnp.sum(gp * pf, axis=1, keepdims=True))).astype(BF16)
                a, b, d = mm(gs, k * masks[h]), mm(gs, q * masks[h], TN), mm(pr, gom, TN)
                gq, gk, gv = (a, b, d) if gq is None else (gq + a, gk + b, gv + d)
            for i, w in enumerate((gq * 0.125, gk * 0.125, gv)):
                self.gst[r, :, pl.ds(pl.multiple_of(p * 128 + i * H, 128), 128)] = w.astype(BF16)
            return c
        tiles(step, 3)
        for row, c in ((5, 0), (6, 2)):
            self.psum[row:row + 1, self.own] += jnp.sum(self.gst[r, :, c * H:(c + 1) * H].astype(F32), axis=0, keepdims=True)

    def project_back(self, r):
        po = mm(self.gst[r], self.wall_rows(1 - self.mp, QKV, 1152), NT)
        pw = mm(self.gst[r], self.wall_rows(self.mp, QKV, 1152), NT)
        self.b_own[r, :, 0:H] = po.astype(BF16)
        self.pown[r] = pw
        so = po * self.par[0:1, self.oth]
        sw = pw * self.par[0:1, self.own]
        s1 = jnp.sum(so + sw, axis=1, keepdims=True)
        s2 = jnp.sum(so * self.xh0[r, :, self.oth] + sw * self.xh0[r, :, self.own], axis=1, keepdims=True)
        lane = lax.broadcasted_iota(jnp.int32, (T, 128), 1)
        st = jnp.where(lane == 0, s1, jnp.where(lane == 1, s2, 0.0))
        self.st[r] = st
        st = jnp.concatenate([st, jnp.zeros((L - T, 128), F32)], axis=0).T
        self.st_own[r] = st[0:8, :]

    def norm_first_back(self, r):
        stp = jnp.concatenate([self.st_peer[r], jnp.zeros((120, L), F32)], axis=0).T[:T]
        self.st[r] += stp
        gain = self.par[0:1, :]

        def tile(i, c):
            g1 = self.sn[r, at(i), :]
            sc1 = g1 * gain
            st = self.st[r, at(i), :]
            m1 = (jnp.sum(sc1, axis=1, keepdims=True) + st[:, 0:1]) * (1.0 / D)
            m2 = (jnp.sum(sc1 * self.xh0[r, at(i), :], axis=1, keepdims=True) + st[:, 1:2]) * (1.0 / D)
            xh = self.xh0[r, at(i), self.own]
            e = self.sn[r, at(i), self.own] + self.pown[r, at(i), :] + self.b_peer[r, at(i), 0:H].astype(F32)
            g = self.inv0[r, at(i), :] * (e * self.par[0:1, self.own] - m1 - xh * m2)
            self.gf[r, at(i), :] = g
            low = (g * self.dconv[r, at(i), :]).astype(BF16)
            lf = low.astype(F32)
            self.dconv[r, at(i), :] = lf
            sums = [jnp.sum(w, axis=0, keepdims=True) for w in (e * xh, e, lf)]
            return tuple(x + y for x, y in zip(c, sums))
        z = jnp.zeros((1, H), F32)
        s = tiles(tile, init=(z, z, z))
        for row, val in zip((0, 4, 3), s):
            self.psum[row:row + 1, self.own] += val
        self.turn_in(self.gt, r, self.dconv[r])

    def conv_backward(self):
        def group(g, c):
            self.shift_inputs(g)
            for r in range(R):
                gg = self.gt[r, at(g, GW), :]
                for b in range(NB):
                    v = pltpu.roll(gg, b, axis=1) if b else gg
                    self.g8[b * GW:(b + 1) * GW, r * L:(r + 1) * L] = v.astype(BF16)
            w = self.convw[:, at(g, GW), :].reshape(NA * GW, NB * GW)
            z = mm(w, self.g8[...])
            for r in range(R):
                acc = None
                for a in range(NA):
                    sh = (8 * a - 64) % L
                    v = z[a * GW:(a + 1) * GW, r * L:(r + 1) * L]
                    v = pltpu.roll(v, sh, axis=1) if sh else v
                    acc = v if acc is None else acc + v
                self.ot[r, at(g, GW), :] = acc
            gr = mm(self.x16[...], self.g8[...], NT)
            self.convw[:, at(g, GW), :] = gr.reshape(NA, GW, NB * GW).astype(BF16)
            return c
        tiles(group, 8)
        for r in range(R):
            self.gf[r] += self.ot[r].T[:T] * self.live[r].astype(F32)

SCRATCH = dict(
    convw=((16, H, H), BF16), wall=((16, 48, 4608), BF16),
    xt=((R, H, L), F32), ot=((R, H, L), F32), gt=((R, H, L), F32), x16=((768, R * L), BF16), g8=((H, R * L), BF16),
    gc=((R, T, D), BF16), dconv=((R, T, H), F32), xh0=((R, T, D), F32), inv0=((R, T, 1), F32), fn=((R, T, D), F32), flow=((R, T, D), BF16),
    qkv=((R, T, 1152), BF16), prob=((R * 6, T, T), BF16), ctx=((R, T, H), BF16),
    a_own=((R, T, D), BF16), a_peer=((R, T, D), BF16), b_own=((R, T, D), BF16), b_peer=((R, T, D), BF16),
    xh1=((R, T, D), F32), inv1=((R, T, 1), F32), sn=((R, T, D), F32), slow=((R, T, D), BF16),
    hid=((R, T, FF), BF16), dg=((R, T, FF), BF16), mixf=((T, D), BF16), gdl=((R, T, D), BF16), gal=((R, T, D), BF16),
    gctx=((R, T, H), BF16), gst=((R, T, 1152), BF16), pown=((R, T, H), F32), st=((R, T, 128), F32),
    st_own=((R, 8, L), F32), st_peer=((R, 8, L), F32), psum=((16, D), F32),
)
INS = ("convw_hbm", "wa_hbm", "wb_hbm", "act", "par", "upb", "segq", "segk", "live")
OUTS = ("mixed", "gf", "gconv_hbm", "ga_hbm", "gb_hbm", "pout")

def mid_kernel(*refs):
    m = Mid()
    names = INS + OUTS + tuple(SCRATCH)
    for name, ref in zip(names, refs):
        setattr(m, name, ref)
    loc, snd, rcv = refs[len(names):]
    mp = lax.axis_index("mp")
    m.mp = mp
    m.own = pl.ds(pl.multiple_of(mp * H, 128), H)
    m.oth = pl.ds(pl.multiple_of((1 - mp) * H, 128), H)
    loads = [pltpu.make_async_copy(m.convw_hbm, m.convw, loc.at[0]), pltpu.make_async_copy(m.wa_hbm, m.wall.at[:, :, 0:UP], loc.at[1]), pltpu.make_async_copy(m.wb_hbm, m.wall.at[:, :, UP:4608], loc.at[2])]
    for c in loads:
        c.start()
    peer = {"mp": 1 - mp}
    bar = pltpu.get_barrier_semaphore()
    pl.semaphore_signal(bar, inc=1, device_id=peer, device_id_type=MESH)
    m.psum[...] = jnp.zeros((16, D), F32)
    m.pout[...] = jnp.zeros((16, H), F32)
    pl.semaphore_wait(bar, 1)

    def swap(i, r, src, dst, land):
        c = pltpu.make_async_remote_copy(src, dst, snd.at[i, r], rcv.at[i, r], device_id=peer, device_id_type=MESH)
        c.start()
        return c, pltpu.make_async_remote_copy(land, land, snd.at[i, r], rcv.at[i, r], device_id=peer, device_id_type=MESH)

    loads[0].wait()
    m.conv_forward()
    pend = {}
    for r in range(R):
        m.conv_finish(r)
        pend[0, r] = swap(0, r, m.gc.at[r, :, m.own], m.gc.at[r, :, m.own], m.gc.at[r, :, m.oth])
    loads[1].wait()
    loads[2].wait()
    for r in range(R):
        pend[0, r][1].wait_recv()
        m.norm_first(r)
        m.project(r)
        m.attend(r)
        pend[1, r] = swap(1, r, m.a_own.at[r], m.a_peer.at[r], m.a_peer.at[r])
    for r in range(R):
        pend[1, r][1].wait_recv()
        m.norm_second(r)
        m.feed_forward(r)
        pend[2, r] = swap(2, r, m.b_own.at[r], m.b_peer.at[r], m.b_peer.at[r])
    for r in range(R):
        pend[2, r][1].wait_recv()
        m.norm_third(r)
        pend[1, r][0].wait_send()
        m.feed_backward(r)
        pend[3, r] = swap(3, r, m.a_own.at[r], m.a_peer.at[r], m.a_peer.at[r])
    m.weight_grad(m.gdl, m.hid, 4, DOWN)
    m.weight_grad(m.slow, m.dg, 4, UP)
    gb = pltpu.make_async_copy(m.wall.at[:, :, UP:4608], m.gb_hbm, loc.at[2])
    gb.start()
    for r in range(R):
        pend[3, r][1].wait_recv()
        m.norm_second_back(r)
        m.attend_back(r)
        pend[2, r][0].wait_send()
        m.project_back(r)
        pend[4, r] = swap(4, r, m.b_own.at[r, :, 0:H], m.b_peer.at[r, :, 0:H], m.b_peer.at[r, :, 0:H])
        pend[5, r] = swap(5, r, m.st_own.at[r], m.st_peer.at[r], m.st_peer.at[r])
    m.weight_grad(m.gal, m.ctx, 1, OUT)
    m.weight_grad(m.flow, m.gst, 3, QKV)
    ga = pltpu.make_async_copy(m.wall.at[:, :, 0:UP], m.ga_hbm, loc.at[1])
    ga.start()
    for r in range(R):
        pend[5, r][1].wait_recv()
        pend[4, r][1].wait_recv()
        m.norm_first_back(r)
    m.conv_backward()
    gc = pltpu.make_async_copy(m.convw, m.gconv_hbm, loc.at[0])
    gc.start()
    m.pout[0:11, :] = m.psum[0:11, m.own]
    for i, r in ((0, 0), (0, 1), (3, 0), (3, 1), (4, 0), (4, 1), (5, 0), (5, 1)):
        pend[i, r][0].wait_send()
    ga.wait()
    gb.wait()
    gc.wait()

def mid(convw, wa, wb, act, par, upb, segq, segk, live):
    vm, hb = pl.BlockSpec(memory_space=pltpu.VMEM), pl.BlockSpec(memory_space=pl.ANY)
    return pl.pallas_call(
        mid_kernel,
        out_shape=[jax.ShapeDtypeStruct((R, T, H), BF16), jax.ShapeDtypeStruct((R, T, H), F32), jax.ShapeDtypeStruct((16, H, H), BF16),
                   jax.ShapeDtypeStruct((16, 48, UP), BF16), jax.ShapeDtypeStruct((16, 48, 4608 - UP), BF16), jax.ShapeDtypeStruct((16, H), F32)],
        in_specs=[hb] * 3 + [vm] * 6,
        out_specs=[vm, vm, hb, hb, hb, vm],
        scratch_shapes=[pltpu.VMEM(s, d) for s, d in SCRATCH.values()] + [pltpu.SemaphoreType.DMA((3,)), pltpu.SemaphoreType.DMA((6, R)), pltpu.SemaphoreType.DMA((6, R))],
        compiler_params=pltpu.CompilerParams(collective_id=1, has_side_effects=True, vmem_limit_bytes=60 << 20),
        name="layer",
    )(convw, wa, wb, act, par, upb, segq, segk, live)


def ring_place(n):
    me = lax.axis_index("dp")
    core = lax.rem(me, 2)
    chip = me // 2
    odd = lax.rem(chip, 2)
    half = chip // 2
    pos = (1 - odd) * half + odd * (n - 1 - half)
    step = 1 - 2 * core
    def dev_at(p, c):
        p = lax.rem(p + 8 * n, n)
        q = p // (n // 2)
        return 2 * ((1 - q) * 2 * p + q * (2 * (n - 1 - p) + 1)) + c
    return me, core, pos, step, dev_at

def ag_kernel(n, ns, *refs):
    shards, (act, par), fulls, (act_full, par_full), sems = refs[:ns], refs[ns:ns+2], refs[ns+2:2*ns+2], refs[2*ns+2:2*ns+4], refs[2*ns+4:]
    ring_s, ring_r, sib_s, sib_r, loc, mp_s, mp_r = sems
    me, core, pos, step, dev_at = ring_place(n)
    mp = lax.axis_index("mp")
    nxt, prv, sib = dev_at(pos + step, core), dev_at(pos - step, core), me + 1 - 2 * core
    bar = pltpu.get_barrier_semaphore()
    for d in ({"dp": nxt}, {"dp": prv}, {"dp": sib}, {"mp": 1 - mp}):
        pl.semaphore_signal(bar, inc=1, device_id=d, device_id_type=MESH)
    pl.semaphore_wait(bar, 4)
    W = act.shape[-1]
    cols = pl.ds(pl.multiple_of(mp * W, 128), W)
    mps = [pltpu.make_async_remote_copy(act, act_full.at[:, :, :, cols], mp_s.at[0], mp_r.at[0], device_id={"mp": 1 - mp}, device_id_type=MESH),
           pltpu.make_async_remote_copy(par, par_full.at[:, cols], mp_s.at[1], mp_r.at[1], device_id={"mp": 1 - mp}, device_id_type=MESH)]
    for c in mps: c.start()
    locs = [pltpu.make_async_copy(act, act_full.at[:, :, :, cols], loc.at[ns]), pltpu.make_async_copy(par, par_full.at[:, cols], loc.at[ns + 1])]
    for i in range(ns):
        locs.append(pltpu.make_async_copy(shards[i], fulls[i].at[me], loc.at[i]))
    for c in locs: c.start()
    started = []
    for s in range(n):
        mine = dev_at(pos - step * s, core)
        for i in range(ns):
            slot = fulls[i].at[mine]
            src = shards[i] if s == 0 else slot
            if s > 0:
                pltpu.make_async_remote_copy(slot, slot, ring_s.at[i, s - 1], ring_r.at[i, s - 1], device_id={"dp": nxt}, device_id_type=MESH).wait_recv()
            if s < n - 1:
                c = pltpu.make_async_remote_copy(src, slot, ring_s.at[i, s], ring_r.at[i, s], device_id={"dp": nxt}, device_id_type=MESH)
                c.start(); started.append(c)
            c = pltpu.make_async_remote_copy(src, slot, sib_s.at[i, s], sib_r.at[i, s], device_id={"dp": sib}, device_id_type=MESH)
            c.start(); started.append(c)
    for c in started: c.wait_send()
    for s in range(n):
        theirs = dev_at(pos + step * s, 1 - core)
        for i in range(ns):
            slot = fulls[i].at[theirs]
            pltpu.make_async_remote_copy(slot, slot, sib_s.at[i, s], sib_r.at[i, s], device_id={"dp": sib}, device_id_type=MESH).wait_recv()
    for c in locs: c.wait()
    ocols = pl.ds(pl.multiple_of((1 - mp) * W, 128), W)
    for c in mps: c.wait_send()
    for i, d in enumerate((act_full.at[:, :, :, ocols], par_full.at[:, ocols])):
        pltpu.make_async_remote_copy(d, d, mp_s.at[i], mp_r.at[i], device_id={"mp": 1 - mp}, device_id_type=MESH).wait_recv()

def ag(shards, act, par, ndp):
    n = ndp // 2
    ns = len(shards)
    hb = pl.BlockSpec(memory_space=pl.ANY)
    outs = [jax.ShapeDtypeStruct((ndp,) + s.shape, s.dtype) for s in shards]
    outs += [jax.ShapeDtypeStruct(act.shape[:-1] + (2 * act.shape[-1],), act.dtype), jax.ShapeDtypeStruct((par.shape[0], 2 * par.shape[1]), par.dtype)]
    return pl.pallas_call(functools.partial(ag_kernel, n, ns), out_shape=outs, in_specs=[hb] * (ns + 2), out_specs=[hb] * (ns + 2),
        scratch_shapes=[pltpu.SemaphoreType.DMA((ns, n)), pltpu.SemaphoreType.DMA((ns, n)), pltpu.SemaphoreType.DMA((ns, n)), pltpu.SemaphoreType.DMA((ns, n)),
                        pltpu.SemaphoreType.DMA((ns + 2,)), pltpu.SemaphoreType.DMA((2,)), pltpu.SemaphoreType.DMA((2,))],
        compiler_params=pltpu.CompilerParams(collective_id=0, has_side_effects=True), name="gather")(*shards, act, par)


def rs_kernel(n, ns, *refs):
    gins, par, outs, par_out = refs[:ns], refs[ns], refs[ns + 1:2 * ns + 1], refs[2 * ns + 1]
    k = 2 * ns + 2
    owns, sibs, rrs = refs[k:k + ns], refs[k + ns:k + 2 * ns], refs[k + 2 * ns:k + 3 * ns]
    pall, ring_s, ring_r, sib_s, sib_r, loc = refs[k + 3 * ns:]
    me, core, pos, step, dev_at = ring_place(n)
    nxt, prv, sib = dev_at(pos + step, core), dev_at(pos - step, core), me + 1 - 2 * core
    bar = pltpu.get_barrier_semaphore()
    for d in (nxt, prv, sib):
        pl.semaphore_signal(bar, inc=1, device_id={"dp": d}, device_id_type=MESH)
    def rc(src, dst, s, r, d):
        return pltpu.make_async_remote_copy(src, dst, s, r, device_id={"dp": d}, device_id_type=MESH)
    loads = {}
    for j in range(n):
        for i in range(ns):
            c = pltpu.make_async_copy(gins[i].at[dev_at(pos - step * (1 + j), core)], owns[i].at[j], loc.at[i, j])
            c.start(); loads[i, j] = c
    pall[pl.ds(me, 1)] = par[...][None]
    pl.semaphore_wait(bar, 3)
    sends = []
    for j in range(n):
        for i in range(ns):
            c = rc(gins[i].at[dev_at(pos + step * (1 + j), 1 - core)], sibs[i].at[j], sib_s.at[i, j], sib_r.at[i, j], sib)
            c.start(); sends.append(c)
    for j in range(n):
        mine = dev_at(pos - step * j, core)
        slot = pall.at[pl.ds(mine, 1)]
        if j > 0:
            rc(slot, slot, ring_s.at[ns, j - 1], ring_r.at[ns, j - 1], nxt).wait_recv()
        if j < n - 1:
            c = rc(slot, slot, ring_s.at[ns, j], ring_r.at[ns, j], nxt)
            c.start(); sends.append(c)
        c = rc(slot, slot, sib_s.at[ns, j], sib_r.at[ns, j], sib)
        c.start(); sends.append(c)
        for i in range(ns):
            loads[i, j].wait()
            sb = sibs[i].at[j]
            rc(sb, sb, sib_s.at[i, j], sib_r.at[i, j], sib).wait_recv()
            if j > 0:
                rb = rrs[i].at[j - 1]
                rc(rb, rb, ring_s.at[i, j - 1], ring_r.at[i, j - 1], nxt).wait_recv()
            rows, cols = owns[i].shape[1:]
            tm = 16
            def tile(t, c, i=i, j=j):
                at = pl.ds(pl.multiple_of(t * tm, tm), tm)
                v = owns[i][j, at, :].astype(F32) + sibs[i][j, at, :].astype(F32)
                if j > 0:
                    v = v + rrs[i][j - 1, at, :].astype(F32)
                if j < n - 1:
                    sibs[i][j, at, :] = v.astype(BF16)
                else:
                    outs[i][at, :] = v
                return c
            lax.fori_loop(0, rows // tm, tile, 0)
            if j < n - 1:
                c = rc(sibs[i].at[j], rrs[i].at[j], ring_s.at[i, j], ring_r.at[i, j], nxt)
                c.start(); sends.append(c)
    for j in range(n):
        slot = pall.at[pl.ds(dev_at(pos + step * j, 1 - core), 1)]
        rc(slot, slot, sib_s.at[ns, j], sib_r.at[ns, j], sib).wait_recv()
    par_out[...] = jnp.sum(pall[...], axis=0)
    for c in sends:
        c.wait_send()

def rs(gins, par, ndp):
    n, ns = ndp // 2, len(gins)
    hb, vm = pl.BlockSpec(memory_space=pl.ANY), pl.BlockSpec(memory_space=pltpu.VMEM)
    sh = [g.shape[1:] for g in gins]
    return pl.pallas_call(functools.partial(rs_kernel, n, ns),
        out_shape=[jax.ShapeDtypeStruct(s, F32) for s in sh] + [jax.ShapeDtypeStruct(par.shape, F32)],
        in_specs=[hb] * ns + [vm], out_specs=[vm] * (ns + 1),
        scratch_shapes=[pltpu.VMEM((n,) + s, BF16) for s in sh] * 2 + [pltpu.VMEM((n - 1,) + s, BF16) for s in sh]
            + [pltpu.VMEM((ndp,) + par.shape, F32)] + [pltpu.SemaphoreType.DMA((ns + 1, n))] * 4 + [pltpu.SemaphoreType.DMA((ns, n))],
        compiler_params=pltpu.CompilerParams(collective_id=2, has_side_effects=True, vmem_limit_bytes=48 << 20), name="scatter")(*gins, par)


def taps_in(weight):
    blocks = weight.reshape(-1, 8, 48, 8, 48)
    return blocks.transpose(0, 3, 2, 1, 4).reshape(-1, 384, 384)


def taps_out(grad):
    blocks = grad.reshape(-1, 8, 48, 8, 48)
    return blocks.transpose(0, 3, 2, 1, 4).reshape(-1, 384)


def body(ndp, frames, segment_ids, live, conv_weight, qkv_weight, out_weight, up_weight, down_weight,
         up_bias, gains, biases, out_grad):
    regular = conv_weight.shape[0] == 384 and qkv_weight.shape[0] == 48
    wa = jnp.concatenate([qkv_weight.reshape(-1, 3 * H), out_weight.T], axis=1)
    wb = jnp.concatenate([up_weight, down_weight.T], axis=1)
    act = jnp.stack([frames, out_grad])
    par = jnp.concatenate([gains, biases, jnp.zeros((5, H), F32)], axis=0)
    if regular:
        convw, wa, wb, act, par = ag((taps_in(conv_weight)[0], wa, wb), act, par, ndp)
    else:
        convw = taps_in(lax.all_gather(conv_weight, "dp", axis=0, tiled=True))
        wa, wb = (lax.all_gather(w, "dp", axis=0, tiled=True).reshape(16, 48, -1) for w in (wa, wb))
        act, par = (lax.all_gather(w, "mp", axis=w.ndim - 1, tiled=True) for w in (act, par))
    mixed, grad_in, g_conv, g_a, g_b, sums = mid(
        convw, wa, wb, act, par, up_bias[None], segment_ids[:, :, None], segment_ids[:, None], live[:, :, None]
    )
    if regular:
        g_conv, g_a, g_b, sums = rs((g_conv, g_a, g_b), sums, ndp)
        g_conv = taps_out(g_conv)
    else:
        g_conv, g_a, g_b = (
            lax.psum_scatter(g, "dp", scatter_dimension=0, tiled=True).astype(F32)
            for g in (taps_out(g_conv), g_a.reshape(D, -1), g_b.reshape(D, -1))
        )
        sums = lax.psum(sums, "dp")
    return (
        mixed,
        grad_in,
        g_conv,
        g_a[:, :1152].reshape(-1, 3, H),
        g_a[:, 1152:].T,
        g_b[:, :FF],
        g_b[:, FF:].T,
        sums[12:16].reshape(FF),
        sums[0:3],
        sums[3:11],
    )


def solution(mesh):
    placed = (
        P("dp", None, "mp"),
        P("dp", None),
        P("dp", None),
        P("dp", "mp"),
        P("dp", None, "mp"),
        P("mp", "dp"),
        P("dp", "mp"),
        P("mp", "dp"),
        P("mp"),
        P(None, "mp"),
        P(None, "mp"),
        P("dp", None, "mp"),
    )
    return jax.shard_map(
        functools.partial(body, mesh.shape["dp"]),
        mesh=mesh,
        in_specs=placed,
        out_specs=(
            P("dp", None, "mp"),
            P("dp", None, "mp"),
            P("dp", "mp"),
            P("dp", None, "mp"),
            P("mp", "dp"),
            P("dp", "mp"),
            P("mp", "dp"),
            P("mp"),
            P(None, "mp"),
            P(None, "mp"),
        ),
        check_vma=False,
    )
```

time: 1770 us -> 281 us (0.16)
  matrix products: 1080 us -> 0 us
  local copies, waits for them, and re-layouts: 320 us -> 23.7 us
  Pallas kernels: 0 us -> 250 us
  blocking collectives: 187 us -> 0 us
  waiting for transfers between devices: 111 us -> 0 us
  other arithmetic: 39.1 us -> 5.68 us
    conv_general_dilated x6 -> x0, matrix products: 922 us -> none  [the longest x2 496 us: conv_weight_grad(): lax.conv_general_dilated(left_side, right_side, (1,), [(0, 0)], dimension...]
    pallas_call x0 -> x3, Pallas kernels: none -> 250 us  [the longest x1 122 us: mid(): pl.pallas_call(mid_kernel, out_shape=[jax.ShapeDtypeStruct((R, T, H), BF1...]
    dot_general x108 -> x0, matrix products: 157 us -> none  [the longest x24 28.1 us: masked_scores(): jnp.einsum('qe,ke->qk', queries, keys_low, preferred_element_type=jnp.flo...]
    psum x10 -> x0, blocking collectives: 105 us -> none  [the longest x1 57.7 us: body(): lax.psum((gain_sums, bias_sums, up_bias_sum), 'dp')]
    rev x2 -> x0, local copies, waits for them, and re-layouts: 88 us -> none  [conv_input_grad(): kernel.reshape(tap_count, group_width, group_count, group_width)]
    all_gather x9 -> x0, blocking collectives: 82.7 us -> none  [the longest x4 27.8 us: spread_features(): lax.all_gather(features.astype(jnp.bfloat16), 'mp', axis=2, tiled=True)]
    all_gather x4 -> x0, waiting for transfers between devices: 73.3 us -> none  [the longest x1 35.5 us: fetch(): lax.all_gather(down_weight, 'dp', axis=1, tiled=True)]
    unnamed x356 -> x14, local copies, waits for them, and re-layouts: 71.5 us -> 4.13 us
  transfers between devices with their start and end apart: 17 -> 0, of which waited for: 6 -> 0; matrix products, arithmetic and copies ran while one was open for 74% -> 0% of each run, Pallas kernels for 0% -> 0%
where the time goes in v2:
time: 281 us; the launch traced here: 280 us
  Pallas kernels  250 us (89%)
  local copies, waits for them, and re-layouts  23.7 us (8%)
  other arithmetic  5.68 us (2%)
    pallas_call x1, Pallas kernels, mid(): pl.pallas_call(mid_kernel, out_shape=[jax.ShapeDtypeStruct((R, T, H), BF1...  122 us
    pallas_call x1, Pallas kernels, ag(): pl.pallas_call(functools.partial(ag_kernel, n, ns), out_shape=outs, in_sp...  64.2 us
    pallas_call x1, Pallas kernels, rs(): pl.pallas_call(functools.partial(rs_kernel, n, ns), out_shape=[jax.ShapeD...  64 us

profile of v2, /device:TPU:0, one launch (start us, length us, event | category | flops | bytes accessed | tf_op | source)
XLA Modules:
  0.0 280.1 jit_solution(923585117668090710)
XLA Ops:
  0.7 0.1 pad.2.clone
  0.7 1.3 broadcast_in_dim.18.refs_7_
  2.0 1.3 broadcast_in_dim.16.refs_5_
  3.3 1.4 maximum_maximum_fusion.refs_4_
  4.7 0.9 copy.33
  5.6 1.4 pad_maximum_fusion.2.refs_1_
  7.0 0.0 copy-start.4
  7.0 0.0 copy-start.5
  7.0 1.8 pad_maximum_fusion.1.refs_2_
  8.8 1.6 copy.29.refs_8_
  10.4 1.6 copy.28.refs_6_
  12.0 1.7 reshape.38
  13.7 0.5 copy.36
  14.3 1.2 squeeze_reshape.3.refs_0_
  15.5 0.0 copy-done.4
  15.5 0.0 copy-done.5
  15.5 1.1 pad_maximum_fusion.refs_3_
  16.6 64.2 %gather.1 = (bf16[16,384,384]{2,1,0:T(8,128)(2,1)}, bf16[16,48,1536]{2,1,0:T(8,128)(2,1)}, bf16[16,48,3072]{2,1,0:T(8,128)(2,1)}, bf16[2,2,320,768]{3,2,1,0:T(8,128)(2,1)}, f32[16,768]{1,0:T(8,128)}) custom-call(bf16[384,384]{1,0:T(8,128)(2,1)} %squeeze_reshape.3.refs_0_, bf16[48,1536]{1,0:T(8,128)(2,1)} %pad_maximum_fusion.2.refs_1_, ...), custom_call_target="tpu_custom_call" | custom-call | tf_op jit(solution)/shard_map/gather/pallas_call | solution.py:467
  80.8 121.7 %layer.1 = (bf16[2,320,384]{2,1,0:T(8,128)(2,1)}, f32[2,320,384]{2,1,0:T(8,128)}, bf16[16,384,384]{2,1,0:T(8,128)(2,1)}, bf16[16,48,1536]{2,1,0:T(8,128)(2,1)}, ...) custom-call(bf16[16,384,384]{2,1,0:T(8,128)(2,1)} %get-tuple-element.25.refs_0_, ...), custom_call_target="tpu_custom_call" | custom-call | tf_op jit(solution)/shard_map/layer/pallas_call | solution.py:391
  202.5 0.0 copy-start
  202.5 1.7 copy-done
  204.2 0.0 copy-start.1
  204.2 0.7 copy-done.1
  204.9 64.0 %scatter.1 = (f32[384,384]{1,0:T(8,128)S(1)}, f32[48,1536]{1,0:T(8,128)S(1)}, f32[48,3072]{1,0:T(8,128)S(1)}, f32[16,384]{1,0:T(8,128)S(1)}) custom-call(bf16[16,384,384]{2,1,0:T(8,128)(2,1)} %get-tuple-element.32.refs_0_, bf16[16,48,1536]{2,1,0:T(8,128)(2,1)S(1)} %copy-done, bf16[16,48,3072]{2,1,0:T(8,128)(2,1)} %get-tuple-element.34.refs_2_, ...), custom_call_target="tpu_custom_call" | custom-call | tf_op jit(solution)/shard_map/scatter/pallas_call | solution.py:541
  268.9 0.6 slice.26
  269.5 0.6 slice.27
  270.1 0.6 reshape.43
  270.7 0.6 slice_bitcast_fusion.1
  271.4 0.7 copy.37
  272.1 0.8 slice_bitcast_fusion
  272.9 0.6 reshape.40
  273.5 0.0 copy-start.3
  273.6 2.1 copy.30
  275.6 0.0 copy-start.2
  275.6 2.8 reshape.41
  278.4 0.0 copy-done.3
  278.4 0.8 copy.40
  279.2 0.0 copy-done.2
  279.2 0.9 copy.41
  (3 shorter events, 0.0 us)
Async XLA Ops:
  7.0 8.5 %copy-start.4 = (bf16[2,320,384]{2,1,0:T(8,128)(2,1)S(1)}, bf16[2,320,384]{2,1,0:T(8,128)(2,1)}, u32[]{:S(2)}) copy-start(bf16[2,320,384]{2,1,0:T(8,128)(2,1)} %param.23) | copy-start | bytes 1474564
  7.0 8.5 %copy-start.5 = (bf16[2,320,384]{2,1,0:T(8,128)(2,1)S(1)}, bf16[2,320,384]{2,1,0:T(8,128)(2,1)}, u32[]{:S(2)}) copy-start(bf16[2,320,384]{2,1,0:T(8,128)(2,1)} %param.12) | copy-start | bytes 1474564
  202.5 1.7 copy-start
  204.2 0.7 copy-start.1
  273.5 4.8 %copy-start.3 = (bf16[2,320,384]{2,1,0:T(8,128)(2,1)S(1)}, bf16[2,320,384]{2,1,0:T(8,128)(2,1)}, u32[]{:S(2)}) copy-start(bf16[2,320,384]{2,1,0:T(8,128)(2,1)} %get-tuple-element.72) | copy-start | bytes 1474564
  275.6 3.5 %copy-start.2 = (f32[2,320,384]{2,1,0:T(8,128)S(1)}, f32[2,320,384]{2,1,0:T(8,128)}, u32[]{:S(2)}) copy-start(f32[2,320,384]{2,1,0:T(8,128)} %get-tuple-element.73) | copy-start | bytes 2949124
